TPU v7x, 32 devices: a whole 2x2x4 slice. The times are simulated.
32 devices in a mesh: dom: 16 (over z, y, x), rep: 2 (over core).
Axes of the slice: x: 2, y: 2, z: 4, core: 2. Of those that a mesh axis runs over, the one named last changes fastest.
Arguments:
- features: bfloat16 [8192, 256], P('dom'), may hold values from -6 to 6
- weight: bfloat16 [256, 256], replicated, may hold values from -0.375 to 0.375
- grad_out: bfloat16 [8192, 256], P('dom'), may hold values from -6 to 6
- tiles: bfloat16 [16, 16, 512, 512], P('dom', 'rep'), may hold values from -0.125 to 0.125
- tile_mask: int32 [16, 16], P('dom', 'rep'), may hold values from 0 to 1, as said below
Outputs:
- activated: bfloat16 [8192, 256], P('dom')
- feature_grad: bfloat16 [8192, 256], P('dom')
- weight_grad: float32 [256, 256], replicated
Inputs may be any that keep to these rules, and one draw needn't show every extreme that they name: `tile_mask`: the diagonal tiles (offset 0) are always present; other tiles are sparse, more frequent near the diagonal (small offsets or offsets near 16), and some row blocks hold many more tiles than others.
All inputs are finite; a program needn't handle non-finite values.
Results may differ from a plain program's by a relative error of at most 0.007.
Values may be sent and summed in bfloat16 or wider, within the bound.
A program may use at most 64 MiB of HBM per device.

v0:
```python
import jax
import jax.numpy as jnp
from jax import lax
from jax.sharding import PartitionSpec as P


def shifted_2(block, axis, distance):
    devices = range(lax.axis_size(axis))
    route = [((i - distance) % len(devices), i) for i in devices]
    return lax.ppermute(block, axis, route)


def tile_product(tile, weight_flag, operand, transposed):
    if transposed:
        contraction = (((0,), (0,)), ((), ()))
        out_rows = tile.shape[1]
    else:
        contraction = (((1,), (0,)), ((), ()))
        out_rows = tile.shape[0]

    def compute():
        return lax.dot_general(tile, operand, contraction, preferred_element_type=jnp.float32)

    def skipped():
        return jnp.zeros((out_rows, operand.shape[1]), jnp.float32)

    return lax.cond(weight_flag > 0, compute, skipped)


def shards(features, weight, grad_out, tiles, tile_mask):
    domains = lax.axis_size("dom")
    replicas = lax.axis_size("rep")
    sections = domains // replicas
    replica = lax.axis_index("rep")
    bit_count = replicas.bit_length() - 1
    rows_here = features.shape[0]
    hidden = features.shape[1]
    projected = jnp.dot(features, weight, preferred_element_type=jnp.float32).astype(jnp.bfloat16)
    current = projected
    for level in range(bit_count):
        shifted = shifted_2(current, "dom", sections << level)
        current = jnp.where(replica >> level & 1 == 1, shifted, current)
    partial_value = jnp.zeros((rows_here, hidden), jnp.float32)
    for section in range(sections):
        if section > 0:
            current = shifted_2(current, "dom", 1)
        partial_value = partial_value + tile_product(
            tiles[0, section], tile_mask[0, section], current, False
        )
    total = lax.psum(partial_value, "rep")
    gate_value = jax.nn.sigmoid(total)
    activated = (total * gate_value).astype(jnp.bfloat16)
    score_grad = (
        grad_out.astype(jnp.float32) * gate_value * (1.0 + total * (1.0 - gate_value))
    ).astype(jnp.bfloat16)
    carried = tile_product(tiles[0, sections - 1], tile_mask[0, sections - 1], score_grad, True)
    for section in range(sections - 2, -1, -1):
        carried = shifted_2(carried, "dom", -1)
        carried = carried + tile_product(tiles[0, section], tile_mask[0, section], score_grad, True)
    for level in range(bit_count):
        shifted = shifted_2(carried, "dom", -(sections << level))
        carried = jnp.where(replica >> level & 1 == 1, shifted, carried)
    node_grad = lax.psum(carried, "rep").astype(jnp.bfloat16)
    feature_grad = lax.dot_general(
        node_grad, weight, (((1,), (1,)), ((), ())), preferred_element_type=jnp.float32
    ).astype(jnp.bfloat16)
    scaling = (rows_here * domains) ** (-0.5)
    weight_term = lax.dot_general(
        features, node_grad, (((0,), (0,)), ((), ())), preferred_element_type=jnp.float32
    )
    weight_grad = lax.psum(weight_term, "dom") * scaling
    return (activated, feature_grad, weight_grad)


def solution(mesh):
    placed = (P("dom", None), P(), P("dom", None), P("dom", "rep", None, None), P("dom", "rep"))
    return jax.shard_map(
        shards,
        mesh=mesh,
        in_specs=placed,
        out_specs=(P("dom", None), P("dom", None), P()),
        check_vma=False,
    )
```

profile of v0, /device:TPU:1, one launch (start us, length us, event | category | flops | bytes accessed | tf_op | source)
XLA Modules:
  0.0 383.7 jit_solution(7726568219170581650)
XLA Ops:
  12.5 11.6 %collective-permute-done = bf16[512,256]{1,0:T(8,128)(2,1)S(1)} collective-permute-done((bf16[512,256]{1,0:T(8,128)(2,1)S(1)}, bf16[512,256]{1,0:T(8,128)(2,1)S(1)}, u32[]{:S(2)}, u32[]{:S(2)}) %collective-permute-start) | collective-permute-done | bytes 262176 | tf_op jit(solution)/shard_map/ppermute | solution.py:10
  25.2 10.9 %collective-permute-done.1 = bf16[512,256]{1,0:T(8,128)(2,1)S(1)} collective-permute-done((bf16[512,256]{1,0:T(8,128)(2,1)S(1)}, bf16[512,256]{1,0:T(8,128)(2,1)S(1)}, u32[]{:S(2)}, u32[]{:S(2)}) %collective-permute-start.1) | collective-permute-done | bytes 262176 | tf_op jit(solution)/shard_map/ppermute | solution.py:10
  36.8 9.5 %collective-permute-done.2 = bf16[512,256]{1,0:T(8,128)(2,1)S(1)} collective-permute-done((bf16[512,256]{1,0:T(8,128)(2,1)S(1)}, bf16[512,256]{1,0:T(8,128)(2,1)S(1)}, u32[]{:S(2)}, u32[]{:S(2)}) %collective-permute-start.2) | collective-permute-done | bytes 262176 | tf_op jit(solution)/shard_map/ppermute | solution.py:10
  47.0 8.5 %collective-permute-done.3 = bf16[512,256]{1,0:T(8,128)(2,1)S(1)} collective-permute-done((bf16[512,256]{1,0:T(8,128)(2,1)S(1)}, bf16[512,256]{1,0:T(8,128)(2,1)S(1)}, u32[]{:S(2)}, u32[]{:S(2)}) %collective-permute-start.3) | collective-permute-done | bytes 262176 | tf_op jit(solution)/shard_map/ppermute | solution.py:10
  55.5 8.8 %collective-permute-done.4 = bf16[512,256]{1,0:T(8,128)(2,1)S(1)} collective-permute-done((bf16[512,256]{1,0:T(8,128)(2,1)S(1)}, bf16[512,256]{1,0:T(8,128)(2,1)S(1)}, u32[]{:S(2)}, u32[]{:S(2)}) %collective-permute-start.4) | collective-permute-done | bytes 262176 | tf_op jit(solution)/shard_map/ppermute | solution.py:10
  64.3 8.8 %collective-permute-done.5 = bf16[512,256]{1,0:T(8,128)(2,1)S(1)} collective-permute-done((bf16[512,256]{1,0:T(8,128)(2,1)S(1)}, bf16[512,256]{1,0:T(8,128)(2,1)S(1)}, u32[]{:S(2)}, u32[]{:S(2)}) %collective-permute-start.5) | collective-permute-done | bytes 262176 | tf_op jit(solution)/shard_map/ppermute | solution.py:10
  95.6 27.9 %all-reduce.4.cloned.1.call-done = f32[512,256]{1,0:T(8,128)} async-done(((f32[512,256]{1,0:T(8,128)}), f32[512,256]{1,0:T(8,128)}) %all-reduce.4.cloned.1.call-update) | async-done | bytes 524304 | tf_op jit(solution)/shard_map/psum | solution.py:50
  126.3 5.2 %collective-permute-start.8 = (f32[512,256]{1,0:T(8,128)}, f32[512,256]{1,0:T(8,128)}, u32[]{:S(2)}, u32[]{:S(2)}) collective-permute-start(f32[512,256]{1,0:T(8,128)} %get-tuple-element.176), channel_id=1, source_target_pairs={{2,0},{4,2},{6,4},{8,6},{10,8},{12,10},{14,12},{16,14},{18,16},{20... | collective-permute-start | bytes 1572872 | tf_op jit(solution)/shard_map/ppermute | solution.py:10
  132.3 10.6 %collective-permute-done.8 = f32[512,256]{1,0:T(8,128)} collective-permute-done((f32[512,256]{1,0:T(8,128)}, f32[512,256]{1,0:T(8,128)}, u32[]{:S(2)}, u32[]{:S(2)}) %collective-permute-start.8) | collective-permute-done | bytes 524320 | tf_op jit(solution)/shard_map/ppermute | solution.py:10
  145.0 5.8 %collective-permute-start.9 = (f32[512,256]{1,0:T(8,128)}, f32[512,256]{1,0:T(8,128)}, u32[]{:S(2)}, u32[]{:S(2)}) collective-permute-start(f32[512,256]{1,0:T(8,128)} %add.63), channel_id=1, source_target_pairs={{2,0},{4,2},{6,4},{8,6},{10,8},{12,10},{14,12},{16,14},{18,16},{20... | collective-permute-start | bytes 1572872 | tf_op jit(solution)/shard_map/ppermute | solution.py:10
  151.6 9.7 %collective-permute-done.9 = f32[512,256]{1,0:T(8,128)} collective-permute-done((f32[512,256]{1,0:T(8,128)}, f32[512,256]{1,0:T(8,128)}, u32[]{:S(2)}, u32[]{:S(2)}) %collective-permute-start.9) | collective-permute-done | bytes 524320 | tf_op jit(solution)/shard_map/ppermute | solution.py:10
  163.3 5.8 %collective-permute-start.10 = (f32[512,256]{1,0:T(8,128)}, f32[512,256]{1,0:T(8,128)}, u32[]{:S(2)}, u32[]{:S(2)}) collective-permute-start(f32[512,256]{1,0:T(8,128)} %add.64), channel_id=1, source_target_pairs={{2,0},{4,2},{6,4},{8,6},{10,8},{12,10},{14,12},{16,14},{18,16},{20... | collective-permute-start | bytes 1572872 | tf_op jit(solution)/shard_map/ppermute | solution.py:10
  170.0 8.7 %collective-permute-done.10 = f32[512,256]{1,0:T(8,128)} collective-permute-done((f32[512,256]{1,0:T(8,128)}, f32[512,256]{1,0:T(8,128)}, u32[]{:S(2)}, u32[]{:S(2)}) %collective-permute-start.10) | collective-permute-done | bytes 524320 | tf_op jit(solution)/shard_map/ppermute | solution.py:10
  180.8 5.8 %collective-permute-start.11 = (f32[512,256]{1,0:T(8,128)}, f32[512,256]{1,0:T(8,128)}, u32[]{:S(2)}, u32[]{:S(2)}) collective-permute-start(f32[512,256]{1,0:T(8,128)} %add.65), channel_id=1, source_target_pairs={{2,0},{4,2},{6,4},{8,6},{10,8},{12,10},{14,12},{16,14},{18,16},{20... | collective-permute-start | bytes 1572872 | tf_op jit(solution)/shard_map/ppermute | solution.py:10
  186.6 8.6 %collective-permute-done.11 = f32[512,256]{1,0:T(8,128)} collective-permute-done((f32[512,256]{1,0:T(8,128)}, f32[512,256]{1,0:T(8,128)}, u32[]{:S(2)}, u32[]{:S(2)}) %collective-permute-start.11) | collective-permute-done | bytes 524320 | tf_op jit(solution)/shard_map/ppermute | solution.py:10
  197.1 5.8 %collective-permute-start.12 = (f32[512,256]{1,0:T(8,128)}, f32[512,256]{1,0:T(8,128)}, u32[]{:S(2)}, u32[]{:S(2)}) collective-permute-start(f32[512,256]{1,0:T(8,128)} %add.66), channel_id=1, source_target_pairs={{2,0},{4,2},{6,4},{8,6},{10,8},{12,10},{14,12},{16,14},{18,16},{20... | collective-permute-start | bytes 1572872 | tf_op jit(solution)/shard_map/ppermute | solution.py:10
  203.0 7.7 %collective-permute-done.12 = f32[512,256]{1,0:T(8,128)} collective-permute-done((f32[512,256]{1,0:T(8,128)}, f32[512,256]{1,0:T(8,128)}, u32[]{:S(2)}, u32[]{:S(2)}) %collective-permute-start.12) | collective-permute-done | bytes 524320 | tf_op jit(solution)/shard_map/ppermute | solution.py:10
  211.8 5.8 %collective-permute-start.13 = (f32[512,256]{1,0:T(8,128)S(1)}, f32[512,256]{1,0:T(8,128)}, u32[]{:S(2)}, u32[]{:S(2)}) collective-permute-start(f32[512,256]{1,0:T(8,128)S(1)} %add.67), channel_id=1, source_target_pairs={{2,0},{4,2},{6,4},{8,6},{10,8},{12,10},{14,12},{16,14},{18,16},{20... | collective-permute-start | bytes 1572872 | tf_op jit(solution)/shard_map/ppermute | solution.py:10
  217.7 6.4 %collective-permute-done.13 = f32[512,256]{1,0:T(8,128)} collective-permute-done((f32[512,256]{1,0:T(8,128)S(1)}, f32[512,256]{1,0:T(8,128)}, u32[]{:S(2)}, u32[]{:S(2)}) %collective-permute-start.13) | collective-permute-done | bytes 524320 | tf_op jit(solution)/shard_map/ppermute | solution.py:10
  225.2 6.0 %collective-permute-start.14 = (f32[512,256]{1,0:T(8,128)S(1)}, f32[512,256]{1,0:T(8,128)S(1)}, u32[]{:S(2)}, u32[]{:S(2)}) collective-permute-start(f32[512,256]{1,0:T(8,128)S(1)} %add.68), channel_id=1, source_target_pairs={{2,0},{4,2},{6,4},{8,6},{10,8},{12,10},{14,12},{16,14},{18,16},{20... | collective-permute-start | bytes 1572872 | tf_op jit(solution)/shard_map/ppermute | solution.py:10
  231.2 6.1 %collective-permute-done.14 = f32[512,256]{1,0:T(8,128)S(1)} collective-permute-done((f32[512,256]{1,0:T(8,128)S(1)}, f32[512,256]{1,0:T(8,128)S(1)}, u32[]{:S(2)}, u32[]{:S(2)}) %collective-permute-start.14) | collective-permute-done | bytes 524320 | tf_op jit(solution)/shard_map/ppermute | solution.py:10
  237.5 14.0 %collective-permute-done.15 = f32[512,256]{1,0:T(8,128)S(1)} collective-permute-done((f32[512,256]{1,0:T(8,128)S(1)}, f32[512,256]{1,0:T(8,128)S(1)}, u32[]{:S(2)}, u32[]{:S(2)}) %collective-permute-start.15) | collective-permute-done | bytes 524320 | tf_op jit(solution)/shard_map/ppermute | solution.py:10
  251.6 12.6 %all-reduce.7 = bf16[512,256]{1,0:T(8,128)(2,1)S(1)} all-reduce(f32[512,256]{1,0:T(8,128)S(1)} %broadcast_select_fusion), channel_id=1, replica_groups=mesh['dom'=16,'rep'=2] {'rep'}, use_global_device_ids=true, to_apply=%region_33.34 | all-reduce | flops 131072 | bytes 786432 | tf_op jit(solution)/shard_map/psum | solution.py:63
  266.1 108.8 %all-reduce.6.cloned.1.call-done = f32[256,256]{0,1:T(8,128)} async-done(((f32[256,256]{0,1:T(8,128)}), f32[256,256]{0,1:T(8,128)}) %all-reduce.6.cloned.1.call-update) | async-done | bytes 262160 | tf_op jit(solution)/shard_map/psum | solution.py:71
  (79 shorter events, 54.8 us)
Async XLA Ops:
  7.2 1.0 copy-start
  7.2 116.3 %all-reduce.4.cloned.1.call-start = ((), (), s32[]{:S(2)}) async-start(), calls=%async_computation | async-start | bytes 1048576 | tf_op jit(solution)/shard_map/psum | solution.py:50
  9.3 14.8 %collective-permute-start = (bf16[512,256]{1,0:T(8,128)(2,1)S(1)}, bf16[512,256]{1,0:T(8,128)(2,1)S(1)}, u32[]{:S(2)}, u32[]{:S(2)}) collective-permute-start(bf16[512,256]{1,0:T(8,128)(2,1)S(1)} %convolution_convert_fusion.1), channel_id=1, source_target_pairs={{16,0},{18,2},{20,4},{22,6},{24,8},{26,10},{28,12},{30,14},{0,16},... | collective-permute-start | bytes 786440 | tf_op jit(solution)/shard_map/ppermute | solution.py:10
  24.1 12.0 %collective-permute-start.1 = (bf16[512,256]{1,0:T(8,128)(2,1)S(1)}, bf16[512,256]{1,0:T(8,128)(2,1)S(1)}, u32[]{:S(2)}, u32[]{:S(2)}) collective-permute-start(bf16[512,256]{1,0:T(8,128)(2,1)S(1)} %broadcast_select_fusion.1), channel_id=1, source_target_pairs={{30,0},{0,2},{2,4},{4,6},{6,8},{8,10},{10,12},{12,14},{14,16},{16,... | collective-permute-start | bytes 786440 | tf_op jit(solution)/shard_map/ppermute | solution.py:10
  36.1 10.2 %collective-permute-start.2 = (bf16[512,256]{1,0:T(8,128)(2,1)S(1)}, bf16[512,256]{1,0:T(8,128)(2,1)S(1)}, u32[]{:S(2)}, u32[]{:S(2)}) collective-permute-start(bf16[512,256]{1,0:T(8,128)(2,1)S(1)} %collective-permute-done.1), channel_id=1, source_target_pairs={{30,0},{0,2},{2,4},{4,6},{6,8},{8,10},{10,12},{12,14},{14,16},{16,... | collective-permute-start | bytes 786440 | tf_op jit(solution)/shard_map/ppermute | solution.py:10
  46.2 0.7 copy-start.5
  46.2 9.2 %collective-permute-start.3 = (bf16[512,256]{1,0:T(8,128)(2,1)S(1)}, bf16[512,256]{1,0:T(8,128)(2,1)S(1)}, u32[]{:S(2)}, u32[]{:S(2)}) collective-permute-start(bf16[512,256]{1,0:T(8,128)(2,1)S(1)} %collective-permute-done.2), channel_id=1, source_target_pairs={{30,0},{0,2},{2,4},{4,6},{6,8},{8,10},{10,12},{12,14},{14,16},{16,... | collective-permute-start | bytes 786440 | tf_op jit(solution)/shard_map/ppermute | solution.py:10
  55.5 26.6 %copy-start.4 = (bf16[512,256]{1,0:T(8,128)(2,1)}, bf16[512,256]{1,0:T(8,128)(2,1)S(1)}, u32[]{:S(2)}) copy-start(bf16[512,256]{1,0:T(8,128)(2,1)S(1)} %collective-permute-done.3) | copy-start | bytes 786436
  55.5 8.8 %collective-permute-start.4 = (bf16[512,256]{1,0:T(8,128)(2,1)S(1)}, bf16[512,256]{1,0:T(8,128)(2,1)S(1)}, u32[]{:S(2)}, u32[]{:S(2)}) collective-permute-start(bf16[512,256]{1,0:T(8,128)(2,1)S(1)} %collective-permute-done.3), channel_id=1, source_target_pairs={{30,0},{0,2},{2,4},{4,6},{6,8},{8,10},{10,12},{12,14},{14,16},{16,... | collective-permute-start | bytes 786440 | tf_op jit(solution)/shard_map/ppermute | solution.py:10
  64.3 17.8 %copy-start.3 = (bf16[512,256]{1,0:T(8,128)(2,1)}, bf16[512,256]{1,0:T(8,128)(2,1)S(1)}, u32[]{:S(2)}) copy-start(bf16[512,256]{1,0:T(8,128)(2,1)S(1)} %collective-permute-done.4) | copy-start | bytes 786436
  64.3 8.8 %collective-permute-start.5 = (bf16[512,256]{1,0:T(8,128)(2,1)S(1)}, bf16[512,256]{1,0:T(8,128)(2,1)S(1)}, u32[]{:S(2)}, u32[]{:S(2)}) collective-permute-start(bf16[512,256]{1,0:T(8,128)(2,1)S(1)} %collective-permute-done.4), channel_id=1, source_target_pairs={{30,0},{0,2},{2,4},{4,6},{6,8},{8,10},{10,12},{12,14},{14,16},{16,... | collective-permute-start | bytes 786440 | tf_op jit(solution)/shard_map/ppermute | solution.py:10
  73.1 8.9 %collective-permute-start.6 = (bf16[512,256]{1,0:T(8,128)(2,1)S(1)}, bf16[512,256]{1,0:T(8,128)(2,1)}, u32[]{:S(2)}, u32[]{:S(2)}) collective-permute-start(bf16[512,256]{1,0:T(8,128)(2,1)S(1)} %collective-permute-done.5), channel_id=1, source_target_pairs={{30,0},{0,2},{2,4},{4,6},{6,8},{8,10},{10,12},{12,14},{14,16},{16,... | collective-permute-start | bytes 786440 | tf_op jit(solution)/shard_map/ppermute | solution.py:10
  82.1 9.4 %collective-permute-start.7 = (bf16[512,256]{1,0:T(8,128)(2,1)}, bf16[512,256]{1,0:T(8,128)(2,1)}, u32[]{:S(2)}, u32[]{:S(2)}) collective-permute-start(bf16[512,256]{1,0:T(8,128)(2,1)} %collective-permute-done.6), channel_id=1, source_target_pairs={{30,0},{0,2},{2,4},{4,6},{6,8},{8,10},{10,12},{12,14},{14,16},{16,... | collective-permute-start | bytes 786440 | tf_op jit(solution)/shard_map/ppermute | solution.py:10
  90.6 32.9 %copy-start.2 = (bf16[512,256]{1,0:T(8,128)(2,1)S(1)}, bf16[512,256]{1,0:T(8,128)(2,1)}, u32[]{:S(2)}) copy-start(bf16[512,256]{1,0:T(8,128)(2,1)} %param.39) | copy-start | bytes 786436
  95.5 279.5 %all-reduce.6.cloned.1.call-start = ((), (), s32[]{:S(2)}) async-start(), calls=%async_computation.1 | async-start | bytes 524288 | tf_op jit(solution)/shard_map/psum | solution.py:71
  126.3 16.6 %collective-permute-start.8 = (f32[512,256]{1,0:T(8,128)}, f32[512,256]{1,0:T(8,128)}, u32[]{:S(2)}, u32[]{:S(2)}) collective-permute-start(f32[512,256]{1,0:T(8,128)} %get-tuple-element.176), channel_id=1, source_target_pairs={{2,0},{4,2},{6,4},{8,6},{10,8},{12,10},{14,12},{16,14},{18,16},{20... | collective-permute-start | bytes 1572872 | tf_op jit(solution)/shard_map/ppermute | solution.py:10
  145.0 16.3 %collective-permute-start.9 = (f32[512,256]{1,0:T(8,128)}, f32[512,256]{1,0:T(8,128)}, u32[]{:S(2)}, u32[]{:S(2)}) collective-permute-start(f32[512,256]{1,0:T(8,128)} %add.63), channel_id=1, source_target_pairs={{2,0},{4,2},{6,4},{8,6},{10,8},{12,10},{14,12},{16,14},{18,16},{20... | collective-permute-start | bytes 1572872 | tf_op jit(solution)/shard_map/ppermute | solution.py:10
  163.3 15.4 %collective-permute-start.10 = (f32[512,256]{1,0:T(8,128)}, f32[512,256]{1,0:T(8,128)}, u32[]{:S(2)}, u32[]{:S(2)}) collective-permute-start(f32[512,256]{1,0:T(8,128)} %add.64), channel_id=1, source_target_pairs={{2,0},{4,2},{6,4},{8,6},{10,8},{12,10},{14,12},{16,14},{18,16},{20... | collective-permute-start | bytes 1572872 | tf_op jit(solution)/shard_map/ppermute | solution.py:10
  180.8 14.5 %collective-permute-start.11 = (f32[512,256]{1,0:T(8,128)}, f32[512,256]{1,0:T(8,128)}, u32[]{:S(2)}, u32[]{:S(2)}) collective-permute-start(f32[512,256]{1,0:T(8,128)} %add.65), channel_id=1, source_target_pairs={{2,0},{4,2},{6,4},{8,6},{10,8},{12,10},{14,12},{16,14},{18,16},{20... | collective-permute-start | bytes 1572872 | tf_op jit(solution)/shard_map/ppermute | solution.py:10
  197.1 13.5 %collective-permute-start.12 = (f32[512,256]{1,0:T(8,128)}, f32[512,256]{1,0:T(8,128)}, u32[]{:S(2)}, u32[]{:S(2)}) collective-permute-start(f32[512,256]{1,0:T(8,128)} %add.66), channel_id=1, source_target_pairs={{2,0},{4,2},{6,4},{8,6},{10,8},{12,10},{14,12},{16,14},{18,16},{20... | collective-permute-start | bytes 1572872 | tf_op jit(solution)/shard_map/ppermute | solution.py:10
  211.8 12.3 %collective-permute-start.13 = (f32[512,256]{1,0:T(8,128)S(1)}, f32[512,256]{1,0:T(8,128)}, u32[]{:S(2)}, u32[]{:S(2)}) collective-permute-start(f32[512,256]{1,0:T(8,128)S(1)} %add.67), channel_id=1, source_target_pairs={{2,0},{4,2},{6,4},{8,6},{10,8},{12,10},{14,12},{16,14},{18,16},{20... | collective-permute-start | bytes 1572872 | tf_op jit(solution)/shard_map/ppermute | solution.py:10
  217.7 47.5 %copy-start.1 = (bf16[256,256]{1,0:T(8,128)(2,1)S(1)}, bf16[256,256]{1,0:T(8,128)(2,1)}, u32[]{:S(2)}) copy-start(bf16[256,256]{1,0:T(8,128)(2,1)} %param.38) | copy-start | bytes 393220
  225.2 12.1 %collective-permute-start.14 = (f32[512,256]{1,0:T(8,128)S(1)}, f32[512,256]{1,0:T(8,128)S(1)}, u32[]{:S(2)}, u32[]{:S(2)}) collective-permute-start(f32[512,256]{1,0:T(8,128)S(1)} %add.68), channel_id=1, source_target_pairs={{2,0},{4,2},{6,4},{8,6},{10,8},{12,10},{14,12},{16,14},{18,16},{20... | collective-permute-start | bytes 1572872 | tf_op jit(solution)/shard_map/ppermute | solution.py:10
  237.4 14.1 %collective-permute-start.15 = (f32[512,256]{1,0:T(8,128)S(1)}, f32[512,256]{1,0:T(8,128)S(1)}, u32[]{:S(2)}, u32[]{:S(2)}) collective-permute-start(f32[512,256]{1,0:T(8,128)S(1)} %add.69), channel_id=1, source_target_pairs={{16,0},{18,2},{20,4},{22,6},{24,8},{26,10},{28,12},{30,14},{0,16},... | collective-permute-start | bytes 1572872 | tf_op jit(solution)/shard_map/ppermute | solution.py:10
  (1 other events, 0.7 us)
Sparse Core Ops, SparseCore 0:
  95.6 27.8 all-reduce.3
  265.3 109.6 all-reduce.5
where the time goes:
time: 387 us; the launch traced here: 384 us
  waiting for transfers between devices  269 us (70%)
  starting transfers between devices  44.6 us (12%)
  between operations  19.3 us (5%)
  local copies, waits for them, and re-layouts  18.4 us (5%)
  other arithmetic  16.6 us (4%)
  blocking collectives  12.6 us (3%)
    ppermute x16, waiting for transfers between devices, shifted_2(): return lax.ppermute(block, axis, route)  132 us
    psum x1, waiting for transfers between devices, shards(): weight_grad = lax.psum(weight_term, 'dom') * scaling  109 us
    ppermute x16, starting transfers between devices, shifted_2(): return lax.ppermute(block, axis, route)  44.5 us
    psum x1, waiting for transfers between devices, shards(): total = lax.psum(partial_value, 'rep')  27.9 us
    psum x1, blocking collectives, shards(): node_grad = lax.psum(carried, 'rep').astype(jnp.bfloat16)  12.6 us
    add x7, other arithmetic, shards(): carried + tile_product(tiles[0, section], tile_mask[0, section], score_gr...  10.4 us
    another operation x16, local copies, waits for them, and re-layouts  10.1 us
  transfers between devices with their start and end apart: 18, of which 17 were waited for; matrix products, arithmetic and copies ran while one was open for 4% of the time, Pallas kernels for 0%

commit v1 on v0

--- a/solution.py
+++ b/solution.py
@@ -1,7 +1,15 @@
+import functools
+
 import jax
 import jax.numpy as jnp
 from jax import lax
+from jax.experimental import pallas as pl
+from jax.experimental.pallas import tpu as pltpu
 from jax.sharding import PartitionSpec as P
+
+MESH = pl.DeviceIdType.MESH
+F32 = jnp.float32
+BF16 = jnp.bfloat16
 
 
 def shifted_2(block, axis, distance):
@@ -27,7 +35,7 @@
     return lax.cond(weight_flag > 0, compute, skipped)
 
 
-def shards(features, weight, grad_out, tiles, tile_mask):
+def ring_shards(features, weight, grad_out, tiles, tile_mask):
     domains = lax.axis_size("dom")
     replicas = lax.axis_size("rep")
     sections = domains // replicas
@@ -72,10 +80,483 @@
     return (activated, feature_grad, weight_grad)
 
 
+def layer_kernel(
+    domains, scaling,
+    x_ref, w_ref, g_ref, tiles_hbm, mask_ref,
+    act_ref, fg_ref, wg_ref,
+    tiles, xs, ps, from_b, from_a, from_z, part, part_in, ax, st, ws, w_in, w_full, fg_half,
+    tile_sem, x_recv, x_recv_p, x_send_z, x_send_a, x_send_b, x_send_p,
+    part_send, part_recv,
+    p_recv_p, p_send_p, b_send, b_recv, a_send, a_recv, z_send, z_recv,
+    w_send, w_recv, last_send, last_recv,
+):
+    layers = domains // 4
+    levels = 2 + layers.bit_length() - 1
+    sections = domains // 2
+    half = x_ref.shape[0] // 2
+    hidden = x_ref.shape[1]
+    d = lax.axis_index("dom")
+    c = lax.axis_index("rep")
+    other = 1 - c
+    step_a, step_b = 1 + c, 2 - c
+    z = d // 4
+    a = (d // step_a) % 2
+    b = (d // step_b) % 2
+
+    def block_at(z_, b_, a_):
+        return z_ * 4 + b_ * step_b + a_ * step_a
+
+    dev_a, dev_b = block_at(z, b, 1 - a), block_at(z, 1 - b, a)
+    far = []
+    for level in range(1, layers.bit_length() - 1):
+        dist = 1 << level
+        far.append(block_at(z + dist * (1 - 2 * ((z // dist) % 2)), b, a))
+    dev_z1 = block_at(z + (1 - 2 * (z % 2)), b, a)
+
+    def copy_to(src, dst, send, recv, dom, rep):
+        return pltpu.make_async_remote_copy(
+            src_ref=src, dst_ref=dst, send_sem=send, recv_sem=recv,
+            device_id=(dom, rep), device_id_type=MESH,
+        )
+
+    barrier = pltpu.get_barrier_semaphore()
+    for dom, rep in [(dev_a, c), (dev_b, c), (d, other)] + [(f, c) for f in far]:
+        pl.semaphore_signal(barrier, inc=1, device_id=(dom, rep), device_id_type=MESH)
+
+    @pl.when(z > 0)
+    def _():
+        pl.semaphore_signal(barrier, inc=1, device_id=(d - 4, c), device_id_type=MESH)
+
+    @pl.when(z < layers - 1)
+    def _():
+        pl.semaphore_signal(barrier, inc=1, device_id=(d + 4, c), device_id_type=MESH)
+
+    ends = jnp.where(z > 0, 1, 0) + jnp.where(z < layers - 1, 1, 0)
+    pl.semaphore_wait(barrier, 3 + len(far) + ends)
+
+    def owner(j):
+        return ((d - j + domains) % domains) // sections
+
+    def x_copy_z(j, z_, up):
+        return copy_to(xs.at[j, c], xs.at[j, c], x_send_z.at[up, z_], x_recv.at[j], d - 4 + 8 * up, c)
+
+    def x_copy_a(j, z_):
+        return copy_to(xs.at[j, c], xs.at[j, c], x_send_a.at[z_], x_recv.at[j], dev_a, c)
+
+    def x_copy_b(j, z_, a_):
+        return copy_to(xs.at[j, c], xs.at[j, c], x_send_b.at[z_, a_], x_recv.at[j], dev_b, c)
+
+    def x_copy_p(j):
+        return copy_to(xs.at[j, c], xs.at[j, c], x_send_p.at[j], x_recv_p.at[j], d, other)
+
+    def x_arrive(j):
+        copy_to(xs.at[j, c], xs.at[j, c], x_send_p.at[j], x_recv.at[j], d, other).wait_recv()
+
+        @pl.when(owner(j) != c)
+        def _():
+            x_copy_p(j).start()
+
+    xs[d, 0] = x_ref[pl.ds(0, half), :]
+    xs[d, 1] = x_ref[pl.ds(half, half), :]
+
+    @pl.when(z > 0)
+    def _():
+        x_copy_z(d, z, 0).start()
+
+    @pl.when(z < layers - 1)
+    def _():
+        x_copy_z(d, z, 1).start()
+
+    x_copy_b(d, z, a).start()
+    x_copy_a(d, z).start()
+    tile_copy = pltpu.make_async_copy(tiles_hbm.at[0], tiles, tile_sem)
+    tile_copy.start()
+
+    def layer_of(n):
+        return z + ((n + 1) // 2) * (2 * ((n + 1) % 2) - 1)
+
+    def in_range(z_):
+        return jnp.logical_and(z_ >= 0, z_ < layers)
+
+    def from_layer(n):
+        z_ = layer_of(n)
+
+        @pl.when(in_range(z_))
+        def _():
+            j = block_at(z_, b, a)
+            x_arrive(j)
+
+            @pl.when(jnp.logical_and(z_ < z, z < layers - 1))
+            def _():
+                x_copy_z(j, z_, 1).start()
+
+            @pl.when(jnp.logical_and(z_ > z, z > 0))
+            def _():
+                x_copy_z(j, z_, 0).start()
+
+            x_copy_b(j, z_, a).start()
+            x_copy_a(j, z_).start()
+
+    def from_a_side(n):
+        z_ = layer_of(n)
+
+        @pl.when(in_range(z_))
+        def _():
+            j = block_at(z_, b, 1 - a)
+            x_arrive(j)
+            x_copy_b(j, z_, 1 - a).start()
+
+    def from_b_side(n):
+        z_ = layer_of(n)
+
+        @pl.when(in_range(z_))
+        def _():
+            x_arrive(block_at(z_, 1 - b, a))
+            x_arrive(block_at(z_, 1 - b, 1 - a))
+
+    visits = 2 * layers - 1
+
+    def gather_step(n, carry):
+        @pl.when(n < visits)
+        def _():
+            from_layer(n)
+
+        @pl.when(n >= 2)
+        def _():
+            from_a_side(n - 2)
+
+        return carry
+
+    lax.fori_loop(1, visits + 2, gather_step, 0)
+
+    def gather_end(n, carry):
+        from_b_side(n)
+        return carry
+
+    lax.fori_loop(0, visits, gather_end, 0)
+
+    def wait_partner_x(j, carry):
+        @pl.when(jnp.logical_and(owner(j) == c, j != d))
+        def _():
+            copy_to(xs.at[j, other], xs.at[j, other], x_send_p.at[j], x_recv_p.at[j], d, other).wait_recv()
+
+        return carry
+
+    lax.fori_loop(0, domains, wait_partner_x, 0)
+    tile_copy.wait()
+
+    def flag(o):
+        return jnp.where(mask_ref[0, o] > 0, 1.0, 0.0)
+
+    def part_copy(r):
+        return copy_to(part.at[r], part_in.at[r], part_send.at[r], part_recv.at[r], d, other)
+
+    for r in range(2):
+        part[r] = jnp.zeros((half, hidden), F32)
+
+        def forward(o, carry, r=r):
+            j = (d - c * sections - o + 2 * domains) % domains
+            m = flag(o).astype(BF16)
+            rows = pl.ds(r * half, half)
+            part[r] += jnp.dot(
+                tiles[o, rows, pl.ds(0, half)], xs[j, 0] * m, preferred_element_type=F32
+            ) + jnp.dot(tiles[o, rows, pl.ds(half, half)], xs[j, 1] * m, preferred_element_type=F32)
+            return carry
+
+        lax.fori_loop(0, sections, forward, 0)
+        part_copy(r).start()
+
+    for r in range(2):
+        part_copy(r).wait_recv()
+        rows = pl.ds(r * half, half)
+        ax_here = (part[r] + part_in[r]).astype(BF16)
+        ax[rows, :] = ax_here
+        total = jnp.dot(ax_here, w_ref[...], preferred_element_type=F32)
+        gate = jax.nn.sigmoid(total)
+        act_ref[rows, :] = (total * gate).astype(BF16)
+        score = g_ref[rows, :].astype(F32) * gate * (1.0 + total * (1.0 - gate))
+        st[:, rows] = jnp.transpose(score).astype(BF16)
+
+    quarter = hidden // 2
+    w_peers = [dev_a, dev_b, dev_z1] + far
+    w_peers = w_peers[:levels]
+
+    def w_copy(level):
+        return copy_to(
+            ws.at[level], w_in.at[level], w_send.at[level], w_recv.at[level], w_peers[level], c
+        )
+
+    ws[0] = jnp.dot(
+        st[pl.ds(pl.multiple_of(c * quarter, quarter), quarter), :], ax[...],
+        preferred_element_type=F32,
+    )
+
+    def target_layer(t):
+        return jnp.where(t % 2 == 0, layers - 1 - t // 2, t // 2)
+
+    def piece(k):
+        z_ = target_layer(k // 4)
+        q = k % 4
+        b_ = jnp.where(q < 2, 1 - b, b)
+        a_ = jnp.where(q % 2 == 0, 1 - a, a)
+        return z_, b_, a_, block_at(z_, b_, a_)
+
+    def p_copy(j):
+        return copy_to(ps.at[j, other], ps.at[j, other], p_send_p.at[j], p_recv_p.at[j], d, other)
+
+    def b_copy(z_, a_):
+        return copy_to(
+            ps.at[block_at(z_, 1 - b, a_), c], from_b.at[z_, a_], b_send.at[z_, a_], b_recv.at[z_, a_],
+            dev_b, c,
+        )
+
+    def a_copy(z_):
+        return copy_to(
+            ps.at[block_at(z_, b, 1 - a), c], from_a.at[z_], a_send.at[z_], a_recv.at[z_], dev_a, c
+        )
+
+    def z_copy(z_, up):
+        return copy_to(
+            ps.at[block_at(z_, b, a), c], from_z.at[up, z_], z_send.at[z_], z_recv.at[up, z_],
+            d - 4 + 8 * up, c,
+        )
+
+    def backward(k, carry):
+        z_, b_, a_, j = piece(k)
+
+        @pl.when(owner(j) == c)
+        def _():
+            o = (d - j + domains) % domains - c * sections
+            m = flag(o)
+            for h in range(2):
+                ps[j, h] = (
+                    jnp.dot(st[...], tiles[o, :, pl.ds(h * half, half)], preferred_element_type=F32) * m
+                ).astype(BF16)
+            p_copy(j).start()
+
+            @pl.when(b_ != b)
+            def _():
+                b_copy(z_, a_).start()
+
+        return carry
+
+    lax.fori_loop(0, domains, backward, 0)
+
+    def relay_partner(k, carry):
+        z_, b_, a_, j = piece(k)
+
+        @pl.when(owner(j) != c)
+        def _():
+            copy_to(ps.at[j, c], ps.at[j, c], p_send_p.at[j], p_recv_p.at[j], d, other).wait_recv()
+
+            @pl.when(b_ != b)
+            def _():
+                b_copy(z_, a_).start()
+
+        return carry
+
+    lax.fori_loop(0, domains, relay_partner, 0)
+    w_copy(0).start()
+
+    def stage_a(t):
+        z_ = target_layer(t)
+        b_copy(z_, 1 - a).wait_recv()
+        j = block_at(z_, b, 1 - a)
+        ps[j, c] = (ps[j, c].astype(F32) + from_b[z_, 1 - a].astype(F32)).astype(BF16)
+        a_copy(z_).start()
+
+    def stage_z(t):
+        z_ = target_layer(t)
+        b_copy(z_, a).wait_recv()
+        a_copy(z_).wait_recv()
+        j = block_at(z_, b, a)
+
+        def mine():
+            return ps[j, c].astype(F32) + from_b[z_, a].astype(F32) + from_a[z_].astype(F32)
+
+        @pl.when(z_ == z)
+        def _():
+            part[0] = mine()
+
+        @pl.when(z_ > z)
+        def _():
+            @pl.when(z > 0)
+            def _():
+                z_copy(z_, 1).wait_recv()
+                ps[j, c] = (mine() + from_z[1, z_].astype(F32)).astype(BF16)
+
+            @pl.when(z == 0)
+            def _():
+                ps[j, c] = mine().astype(BF16)
+
+            z_copy(z_, 1).start()
+
+        @pl.when(z_ < z)
+        def _():
+            @pl.when(z < layers - 1)
+            def _():
+                z_copy(z_, 0).wait_recv()
+                ps[j, c] = (mine() + from_z[0, z_].astype(F32)).astype(BF16)
+
+            @pl.when(z == layers - 1)
+            def _():
+                ps[j, c] = mine().astype(BF16)
+
+            z_copy(z_, 0).start()
+
+    for r in range(2):
+        part_copy(r).wait_send()
+
+    stages = max(layers + 1, levels)
+    for t in range(stages):
+        if t < layers:
+            stage_a(t)
+        if 1 <= t <= layers:
+            stage_z(t - 1)
+        if t < levels:
+            w_copy(t).wait_recv()
+            ws[t + 1] = ws[t] + w_in[t]
+            if t + 1 < levels:
+                w_copy(t + 1).start()
+
+    w_full[c] = ws[levels]
+    w_last = copy_to(w_full.at[c], w_full.at[c], last_send.at[0], last_recv.at[0], d, other)
+    w_last.start()
+
+    @pl.when(z > 0)
+    def _():
+        z_copy(z, 1).wait_recv()
+        part[0] += from_z[1, z].astype(F32)
+
+    @pl.when(z < layers - 1)
+    def _():
+        z_copy(z, 0).wait_recv()
+        part[0] += from_z[0, z].astype(F32)
+
+    node = jnp.transpose(part[0]).astype(BF16)
+    fg_half[c] = lax.dot_general(
+        node, w_ref[...], (((1,), (1,)), ((), ())), preferred_element_type=F32
+    ).astype(BF16)
+    f_last = copy_to(fg_half.at[c], fg_half.at[c], last_send.at[1], last_recv.at[1], d, other)
+    f_last.start()
+
+    copy_to(w_full.at[other], w_full.at[other], last_send.at[0], last_recv.at[0], d, other).wait_recv()
+    for h in range(2):
+        wg_ref[:, pl.ds(h * quarter, quarter)] = jnp.transpose(w_full[h]) * scaling
+
+    def drain_p(j, carry):
+        @pl.when(jnp.logical_and(owner(j) != c, j != d))
+        def _():
+            x_copy_p(j).wait_send()
+
+        @pl.when(owner(j) == c)
+        def _():
+            p_copy(j).wait_send()
+
+        return carry
+
+    lax.fori_loop(0, domains, drain_p, 0)
+
+    def drain(z_, carry):
+        @pl.when(jnp.logical_and(z_ <= z, z < layers - 1))
+        def _():
+            x_copy_z(block_at(z_, b, a), z_, 1).wait_send()
+
+        @pl.when(jnp.logical_and(z_ >= z, z > 0))
+        def _():
+            x_copy_z(block_at(z_, b, a), z_, 0).wait_send()
+
+        x_copy_a(block_at(z_, b, a), z_).wait_send()
+        a_copy(z_).wait_send()
+        for a_ in range(2):
+            x_copy_b(block_at(z_, b, a_), z_, a_).wait_send()
+            b_copy(z_, a_).wait_send()
+
+        @pl.when(z_ > z)
+        def _():
+            z_copy(z_, 1).wait_send()
+
+        @pl.when(z_ < z)
+        def _():
+            z_copy(z_, 0).wait_send()
+
+        return carry
+
+    lax.fori_loop(0, layers, drain, 0)
+    for level in range(levels):
+        w_copy(level).wait_send()
+    copy_to(fg_half.at[other], fg_half.at[other], last_send.at[1], last_recv.at[1], d, other).wait_recv()
+    for h in range(2):
+        fg_ref[pl.ds(h * half, half), :] = fg_half[h]
+    w_last.wait_send()
+    f_last.wait_send()
+
+
+def kernel_shards(features, weight, grad_out, tiles, tile_mask):
+    domains = lax.axis_size("dom")
+    layers = domains // 4
+    levels = 2 + layers.bit_length() - 1
+    sections = tiles.shape[1]
+    rows, hidden = features.shape
+    half, quarter = rows // 2, hidden // 2
+    dma = pltpu.SemaphoreType.DMA
+    vmem = pl.BlockSpec(memory_space=pltpu.VMEM)
+    return pl.pallas_call(
+        functools.partial(layer_kernel, domains, float((rows * domains) ** (-0.5))),
+        out_shape=(
+            jax.ShapeDtypeStruct((rows, hidden), BF16),
+            jax.ShapeDtypeStruct((rows, hidden), BF16),
+            jax.ShapeDtypeStruct((hidden, hidden), F32),
+        ),
+        in_specs=[
+            vmem, vmem, vmem,
+            pl.BlockSpec(memory_space=pl.ANY),
+            pl.BlockSpec(memory_space=pltpu.SMEM),
+        ],
+        out_specs=(vmem, vmem, vmem),
+        scratch_shapes=[
+            pltpu.VMEM(tiles.shape[1:], BF16),
+            pltpu.VMEM((domains, 2, half, hidden), BF16),
+            pltpu.VMEM((domains, 2, hidden, half), BF16),
+            pltpu.VMEM((layers, 2, hidden, half), BF16),
+            pltpu.VMEM((layers, hidden, half), BF16),
+            pltpu.VMEM((2, layers, hidden, half), BF16),
+            pltpu.VMEM((2, half, hidden), F32),
+            pltpu.VMEM((2, half, hidden), F32),
+            pltpu.VMEM((rows, hidden), BF16),
+            pltpu.VMEM((hidden, rows), BF16),
+            pltpu.VMEM((levels + 1, quarter, hidden), F32),
+            pltpu.VMEM((levels, quarter, hidden), F32),
+            pltpu.VMEM((2, quarter, hidden), F32),
+            pltpu.VMEM((2, half, hidden), BF16),
+            dma,
+            dma((domains,)), dma((domains,)),
+            dma((2, layers)), dma((layers,)), dma((layers, 2)), dma((domains,)),
+            dma((2,)), dma((2,)),
+            dma((domains,)), dma((domains,)),
+            dma((layers, 2)), dma((layers, 2)),
+            dma((layers,)), dma((layers,)),
+            dma((layers,)), dma((2, layers)),
+            dma((levels,)), dma((levels,)),
+            dma((2,)), dma((2,)),
+        ],
+        compiler_params=pltpu.CompilerParams(
+            collective_id=0, has_side_effects=True, vmem_limit_bytes=40 * 1024 * 1024
+        ),
+        cost_estimate=pl.CostEstimate(
+            flops=4 * sections * rows * rows * hidden,
+            bytes_accessed=2 * sections * rows * rows,
+            transcendentals=rows * hidden,
+        ),
+    )(features, weight, grad_out, tiles, tile_mask)
+
+
 def solution(mesh):
+    domains, replicas = mesh.shape["dom"], mesh.shape["rep"]
+    paired = replicas == 2 and domains >= 8 and domains & (domains - 1) == 0
     placed = (P("dom", None), P(), P("dom", None), P("dom", "rep", None, None), P("dom", "rep"))
     return jax.shard_map(
-        shards,
+        kernel_shards if paired else ring_shards,
         mesh=mesh,
         in_specs=placed,
         out_specs=(P("dom", None), P("dom", None), P()),

time: 387 us -> 90 us (0.23)
  the two profiles are of different devices: /device:TPU:1 before, /device:TPU:11 now
where the time goes in v1:
time: 90 us; the launch traced here: 89.7 us
  Pallas kernels  81.3 us (90%)
  local copies, waits for them, and re-layouts  7.75 us (9%)
    pallas_call x1, Pallas kernels, kernel_shards(): pl.pallas_call(functools.partial(layer_kernel, domains, float((rows * dom...  81.3 us
    unnamed x13, local copies, waits for them, and re-layouts  7.75 us

profile of v1, /device:TPU:11, one launch (start us, length us, event | category | flops | bytes accessed | tf_op | source)
XLA Modules:
  0.0 89.7 jit_solution(4367911875412073815)
XLA Ops:
  0.6 0.0 copy-start
  0.6 2.2 %copy-done = bf16[1,8,512,512]{3,2,1,0:T(8,128)(2,1)S(1)} copy-done((bf16[1,8,512,512]{3,2,1,0:T(8,128)(2,1)S(1)}, bf16[1,8,512,512]{3,2,1,0:T(8,128)(2,1)}, u32[]{:S(2)}) %copy-start) | copy-done | bytes 4194328
  2.8 0.0 copy-start.1
  2.8 0.9 %copy-done.1 = bf16[512,256]{1,0:T(8,128)(2,1)S(1)} copy-done((bf16[512,256]{1,0:T(8,128)(2,1)S(1)}, bf16[512,256]{1,0:T(8,128)(2,1)}, u32[]{:S(2)}) %copy-start.1) | copy-done | bytes 262168
  3.8 0.0 copy-start.2
  3.8 0.9 %copy-done.2 = bf16[512,256]{1,0:T(8,128)(2,1)S(1)} copy-done((bf16[512,256]{1,0:T(8,128)(2,1)S(1)}, bf16[512,256]{1,0:T(8,128)(2,1)}, u32[]{:S(2)}) %copy-start.2) | copy-done | bytes 262168
  4.7 0.0 copy-start.3
  4.7 0.9 %copy-done.3 = bf16[256,256]{1,0:T(8,128)(2,1)S(1)} copy-done((bf16[256,256]{1,0:T(8,128)(2,1)S(1)}, bf16[256,256]{1,0:T(8,128)(2,1)}, u32[]{:S(2)}) %copy-start.3) | copy-done | bytes 131096
  5.6 0.0 copy-start.4
  5.6 0.7 copy-done.4
  6.3 81.3 %shard_map.76 = (bf16[512,256]{1,0:T(8,128)(2,1)S(1)}, bf16[512,256]{1,0:T(8,128)(2,1)S(1)}, f32[256,256]{1,0:T(8,128)S(1)}) custom-call(bf16[512,256]{1,0:T(8,128)(2,1)S(1)} %copy-done.1, bf16[256,256]{1,0:T(8,128)(2,1)S(1)} %copy-done.3, bf16[512,256]{1,0:T(8,128)(2,1)S(1)} %copy-done.2, bf16[1,8,512,512]{3,2,1,0:T(8,128)(2,1)S(1)} %copy-done, ...), custom_call_target="tpu_custom_call" | custom-call | flops 2147483648 | bytes 4194304 | tf_op jit(solution)/shard_map/pallas_call | solution.py:504
  87.6 0.7 copy.11
  88.3 0.7 copy.12
  89.0 0.7 copy.13
Async XLA Ops:
  0.6 2.2 %copy-start = (bf16[1,8,512,512]{3,2,1,0:T(8,128)(2,1)S(1)}, bf16[1,8,512,512]{3,2,1,0:T(8,128)(2,1)}, u32[]{:S(2)}) copy-start(bf16[1,8,512,512]{3,2,1,0:T(8,128)(2,1)} %tiles_hbm.1) | copy-start | bytes 12582916
  2.8 0.9 %copy-start.1 = (bf16[512,256]{1,0:T(8,128)(2,1)S(1)}, bf16[512,256]{1,0:T(8,128)(2,1)}, u32[]{:S(2)}) copy-start(bf16[512,256]{1,0:T(8,128)(2,1)} %x_ref.1) | copy-start | bytes 786436
  3.8 0.9 %copy-start.2 = (bf16[512,256]{1,0:T(8,128)(2,1)S(1)}, bf16[512,256]{1,0:T(8,128)(2,1)}, u32[]{:S(2)}) copy-start(bf16[512,256]{1,0:T(8,128)(2,1)} %g_ref.1) | copy-start | bytes 786436
  4.7 0.9 %copy-start.3 = (bf16[256,256]{1,0:T(8,128)(2,1)S(1)}, bf16[256,256]{1,0:T(8,128)(2,1)}, u32[]{:S(2)}) copy-start(bf16[256,256]{1,0:T(8,128)(2,1)} %w_ref.1) | copy-start | bytes 393220
  5.6 0.7 copy-start.4

commit v2 on v1

--- a/solution.py
+++ b/solution.py
@@ -82,10 +82,10 @@
 
 def layer_kernel(
     domains, scaling,
-    x_ref, w_ref, g_ref, tiles_hbm, mask_ref,
+    x_hbm, w_hbm, g_hbm, tiles_hbm, mask_ref,
     act_ref, fg_ref, wg_ref,
-    tiles, xs, ps, from_b, from_a, from_z, part, part_in, ax, st, ws, w_in, w_full, fg_half,
-    tile_sem, x_recv, x_recv_p, x_send_z, x_send_a, x_send_b, x_send_p,
+    w_ref, g_ref, tiles, xs, ps, from_b, from_a, from_z, part, part_in, ax, st, ws, w_in, w_full, fg_half,
+    own_sem, tile_sem, x_recv, x_recv_p, x_send_z, x_send_a, x_send_b, x_send_p,
     part_send, part_recv,
     p_recv_p, p_send_p, b_send, b_recv, a_send, a_recv, z_send, z_recv,
     w_send, w_recv, last_send, last_recv,
@@ -93,8 +93,8 @@
     layers = domains // 4
     levels = 2 + layers.bit_length() - 1
     sections = domains // 2
-    half = x_ref.shape[0] // 2
-    hidden = x_ref.shape[1]
+    half = x_hbm.shape[0] // 2
+    hidden = x_hbm.shape[1]
     d = lax.axis_index("dom")
     c = lax.axis_index("rep")
     other = 1 - c
@@ -119,6 +119,18 @@
             device_id=(dom, rep), device_id_type=MESH,
         )
 
+    own_copies = [
+        pltpu.make_async_copy(x_hbm.at[pl.ds(h * half, half)], xs.at[d, h], own_sem.at[h])
+        for h in range(2)
+    ]
+    tile_copies = [
+        pltpu.make_async_copy(w_hbm, w_ref, tile_sem.at[0]),
+        pltpu.make_async_copy(g_hbm, g_ref, tile_sem.at[1]),
+        pltpu.make_async_copy(tiles_hbm.at[0], tiles, tile_sem.at[2]),
+    ]
+    for copy in own_copies + tile_copies:
+        copy.start()
+
     barrier = pltpu.get_barrier_semaphore()
     for dom, rep in [(dev_a, c), (dev_b, c), (d, other)] + [(f, c) for f in far]:
         pl.semaphore_signal(barrier, inc=1, device_id=(dom, rep), device_id_type=MESH)
@@ -156,8 +168,8 @@
         def _():
             x_copy_p(j).start()
 
-    xs[d, 0] = x_ref[pl.ds(0, half), :]
-    xs[d, 1] = x_ref[pl.ds(half, half), :]
+    for copy in own_copies:
+        copy.wait()
 
     @pl.when(z > 0)
     def _():
@@ -169,8 +181,6 @@
 
     x_copy_b(d, z, a).start()
     x_copy_a(d, z).start()
-    tile_copy = pltpu.make_async_copy(tiles_hbm.at[0], tiles, tile_sem)
-    tile_copy.start()
 
     def layer_of(n):
         return z + ((n + 1) // 2) * (2 * ((n + 1) % 2) - 1)
@@ -214,56 +224,67 @@
             x_arrive(block_at(z_, 1 - b, a))
             x_arrive(block_at(z_, 1 - b, 1 - a))
 
-    visits = 2 * layers - 1
-
-    def gather_step(n, carry):
-        @pl.when(n < visits)
-        def _():
-            from_layer(n)
-
-        @pl.when(n >= 2)
-        def _():
-            from_a_side(n - 2)
-
-        return carry
-
-    lax.fori_loop(1, visits + 2, gather_step, 0)
-
-    def gather_end(n, carry):
-        from_b_side(n)
-        return carry
-
-    lax.fori_loop(0, visits, gather_end, 0)
-
-    def wait_partner_x(j, carry):
-        @pl.when(jnp.logical_and(owner(j) == c, j != d))
-        def _():
-            copy_to(xs.at[j, other], xs.at[j, other], x_send_p.at[j], x_recv_p.at[j], d, other).wait_recv()
-
-        return carry
-
-    lax.fori_loop(0, domains, wait_partner_x, 0)
-    tile_copy.wait()
-
     def flag(o):
         return jnp.where(mask_ref[0, o] > 0, 1.0, 0.0)
 
+    def product(j):
+        o = (d - j + domains) % domains - c * sections
+        m = flag(o).astype(BF16)
+        x_top, x_low = xs[j, 0] * m, xs[j, 1] * m
+        for r in range(2):
+            rows = pl.ds(r * half, half)
+            part[r] += jnp.dot(
+                tiles[o, rows, pl.ds(0, half)], x_top, preferred_element_type=F32
+            ) + jnp.dot(tiles[o, rows, pl.ds(half, half)], x_low, preferred_element_type=F32)
+
+    def products(n):
+        z_ = layer_of(n)
+
+        def one(q, carry):
+            j = z_ * 4 + q
+
+            @pl.when(owner(j) == c)
+            def _():
+                @pl.when(j != d)
+                def _():
+                    copy_to(
+                        xs.at[j, other], xs.at[j, other], x_send_p.at[j], x_recv_p.at[j], d, other
+                    ).wait_recv()
+
+                product(j)
+
+            return carry
+
+        @pl.when(in_range(z_))
+        def _():
+            lax.fori_loop(0, 4, one, 0)
+
+    visits = 2 * layers - 1
+    for copy in tile_copies:
+        copy.wait()
+    for r in range(2):
+        part[r] = jnp.zeros((half, hidden), F32)
+
+    def gather_step(n, carry):
+        for lag, step in enumerate((from_layer, from_a_side, from_b_side)):
+            at = n - 2 * lag
+
+            @pl.when(jnp.logical_and(at >= (1 if lag == 0 else 0), at < visits))
+            def _():
+                step(at)
+
+        @pl.when(n >= 5)
+        def _():
+            products(n - 5)
+
+        return carry
+
+    lax.fori_loop(1, visits + 5, gather_step, 0)
+
     def part_copy(r):
         return copy_to(part.at[r], part_in.at[r], part_send.at[r], part_recv.at[r], d, other)
 
     for r in range(2):
-        part[r] = jnp.zeros((half, hidden), F32)
-
-        def forward(o, carry, r=r):
-            j = (d - c * sections - o + 2 * domains) % domains
-            m = flag(o).astype(BF16)
-            rows = pl.ds(r * half, half)
-            part[r] += jnp.dot(
-                tiles[o, rows, pl.ds(0, half)], xs[j, 0] * m, preferred_element_type=F32
-            ) + jnp.dot(tiles[o, rows, pl.ds(half, half)], xs[j, 1] * m, preferred_element_type=F32)
-            return carry
-
-        lax.fori_loop(0, sections, forward, 0)
         part_copy(r).start()
 
     for r in range(2):
@@ -378,41 +399,47 @@
         def _():
             part[0] = mine()
 
-        @pl.when(z_ > z)
-        def _():
-            @pl.when(z > 0)
-            def _():
-                z_copy(z_, 1).wait_recv()
-                ps[j, c] = (mine() + from_z[1, z_].astype(F32)).astype(BF16)
-
-            @pl.when(z == 0)
-            def _():
-                ps[j, c] = mine().astype(BF16)
-
+        @pl.when(jnp.logical_and(z_ > z, z == 0))
+        def _():
+            ps[j, c] = mine().astype(BF16)
             z_copy(z_, 1).start()
 
-        @pl.when(z_ < z)
-        def _():
-            @pl.when(z < layers - 1)
-            def _():
-                z_copy(z_, 0).wait_recv()
-                ps[j, c] = (mine() + from_z[0, z_].astype(F32)).astype(BF16)
-
-            @pl.when(z == layers - 1)
-            def _():
-                ps[j, c] = mine().astype(BF16)
-
+        @pl.when(jnp.logical_and(z_ < z, z == layers - 1))
+        def _():
+            ps[j, c] = mine().astype(BF16)
             z_copy(z_, 0).start()
+
+    def stage_relay(t):
+        z_ = target_layer(t)
+        j = block_at(z_, b, a)
+
+        def pass_on(up):
+            z_copy(z_, up).wait_recv()
+            ps[j, c] = (
+                ps[j, c].astype(F32) + from_b[z_, a].astype(F32) + from_a[z_].astype(F32)
+                + from_z[up, z_].astype(F32)
+            ).astype(BF16)
+            z_copy(z_, up).start()
+
+        @pl.when(jnp.logical_and(z_ > z, z > 0))
+        def _():
+            pass_on(1)
+
+        @pl.when(jnp.logical_and(z_ < z, z < layers - 1))
+        def _():
+            pass_on(0)
 
     for r in range(2):
         part_copy(r).wait_send()
 
-    stages = max(layers + 1, levels)
+    stages = max(layers + 2, levels)
     for t in range(stages):
         if t < layers:
             stage_a(t)
         if 1 <= t <= layers:
             stage_z(t - 1)
+        if 2 <= t <= layers + 1:
+            stage_relay(t - 2)
         if t < levels:
             w_copy(t).wait_recv()
             ws[t + 1] = ws[t] + w_in[t]
@@ -508,13 +535,11 @@
             jax.ShapeDtypeStruct((rows, hidden), BF16),
             jax.ShapeDtypeStruct((hidden, hidden), F32),
         ),
-        in_specs=[
-            vmem, vmem, vmem,
-            pl.BlockSpec(memory_space=pl.ANY),
-            pl.BlockSpec(memory_space=pltpu.SMEM),
-        ],
+        in_specs=[pl.BlockSpec(memory_space=pl.ANY)] * 4 + [pl.BlockSpec(memory_space=pltpu.SMEM)],
         out_specs=(vmem, vmem, vmem),
         scratch_shapes=[
+            pltpu.VMEM(weight.shape, BF16),
+            pltpu.VMEM((rows, hidden), BF16),
             pltpu.VMEM(tiles.shape[1:], BF16),
             pltpu.VMEM((domains, 2, half, hidden), BF16),
             pltpu.VMEM((domains, 2, hidden, half), BF16),
@@ -529,7 +554,7 @@
             pltpu.VMEM((levels, quarter, hidden), F32),
             pltpu.VMEM((2, quarter, hidden), F32),
             pltpu.VMEM((2, half, hidden), BF16),
-            dma,
+            dma((2,)), dma((3,)),
             dma((domains,)), dma((domains,)),
             dma((2, layers)), dma((layers,)), dma((layers, 2)), dma((domains,)),
             dma((2,)), dma((2,)),
@@ -541,7 +566,7 @@
             dma((2,)), dma((2,)),
         ],
         compiler_params=pltpu.CompilerParams(
-            collective_id=0, has_side_effects=True, vmem_limit_bytes=40 * 1024 * 1024
+            collective_id=0, has_side_effects=True, vmem_limit_bytes=63 * 1024 * 1024
         ),
         cost_estimate=pl.CostEstimate(
             flops=4 * sections * rows * rows * hidden,

time: 90 us -> 81.8 us (0.909)
  the two profiles are of different devices: /device:TPU:11 before, /device:TPU:1 now
where the time goes in v2:
time: 81.8 us; the launch traced here: 81.5 us
  Pallas kernels  75.9 us (93%)
  local copies, waits for them, and re-layouts  5.01 us (6%)
    pallas_call x1, Pallas kernels, kernel_shards(): pl.pallas_call(functools.partial(layer_kernel, domains, float((rows * dom...  75.9 us
    unnamed x3, local copies, waits for them, and re-layouts  5.01 us

profile of v2, /device:TPU:1, one launch (start us, length us, event | category | flops | bytes accessed | tf_op | source)
XLA Modules:
  0.0 81.5 jit_solution(4414167374435221596)
XLA Ops:
  0.6 75.9 %shard_map.76 = (bf16[512,256]{1,0:T(8,128)(2,1)}, bf16[512,256]{1,0:T(8,128)(2,1)}, f32[256,256]{1,0:T(8,128)}) custom-call(bf16[512,256]{1,0:T(8,128)(2,1)} %x_hbm.1, bf16[256,256]{1,0:T(8,128)(2,1)} %w_hbm.1, bf16[512,256]{1,0:T(8,128)(2,1)} %g_hbm.1, bf16[1,8,512,512]{3,2,1,0:T(8,128)(2,1)} %tiles_hbm.1, s32[1,8]{1,0:T(1,128)} %mask_ref.1), custom_call_target="tpu_custom_call" | custom-call | flops 2147483648 | bytes 4194304 | tf_op jit(solution)/shard_map/pallas_call | solution.py:531
  76.5 1.7 %copy.11 = bf16[512,256]{1,0:T(8,128)(2,1)} copy(bf16[512,256]{1,0:T(8,128)(2,1)} %get-tuple-element.6) | data formatting | bytes 524288
  78.2 1.7 %copy.12 = bf16[512,256]{1,0:T(8,128)(2,1)} copy(bf16[512,256]{1,0:T(8,128)(2,1)} %get-tuple-element.7) | data formatting | bytes 524288
  79.9 1.7 %copy.13 = f32[256,256]{1,0:T(8,128)} copy(f32[256,256]{1,0:T(8,128)} %get-tuple-element.8) | data formatting | bytes 524288

commit v3 on v2

--- a/solution.py
+++ b/solution.py
@@ -84,14 +84,14 @@
     domains, scaling,
     x_hbm, w_hbm, g_hbm, tiles_hbm, mask_ref,
     act_ref, fg_ref, wg_ref,
-    w_ref, g_ref, tiles, xs, ps, from_b, from_a, from_z, part, part_in, ax, st, ws, w_in, w_full, fg_half,
+    w_ref, g_ref, tiles, xs, ps, from_b, from_a, from_z, part, part_in, ax, st, ws, w_in, w_cross, w_cross_in, w_full, fg_half,
     own_sem, tile_sem, x_recv, x_recv_p, x_send_z, x_send_a, x_send_b, x_send_p,
     part_send, part_recv,
     p_recv_p, p_send_p, b_send, b_recv, a_send, a_recv, z_send, z_recv,
     w_send, w_recv, last_send, last_recv,
 ):
     layers = domains // 4
-    levels = 2 + layers.bit_length() - 1
+    folds = layers.bit_length() - 1
     sections = domains // 2
     half = x_hbm.shape[0] // 2
     hidden = x_hbm.shape[1]
@@ -107,11 +107,8 @@
         return z_ * 4 + b_ * step_b + a_ * step_a
 
     dev_a, dev_b = block_at(z, b, 1 - a), block_at(z, 1 - b, a)
-    far = []
-    for level in range(1, layers.bit_length() - 1):
-        dist = 1 << level
-        far.append(block_at(z + dist * (1 - 2 * ((z // dist) % 2)), b, a))
-    dev_z1 = block_at(z + (1 - 2 * (z % 2)), b, a)
+    dev_fold = [block_at(z + (1 << f) * (1 - 2 * ((z // (1 << f)) % 2)), b, a) for f in range(folds)]
+    far = dev_fold[1:]
 
     def copy_to(src, dst, send, recv, dom, rep):
         return pltpu.make_async_remote_copy(
@@ -299,15 +296,60 @@
         st[:, rows] = jnp.transpose(score).astype(BF16)
 
     quarter = hidden // 2
-    w_peers = [dev_a, dev_b, dev_z1] + far
-    w_peers = w_peers[:levels]
-
-    def w_copy(level):
+    sizes, bases = [quarter], [0]
+    for f in range(folds):
+        sizes.append(sizes[-1] // 2)
+        bases.append(bases[-1] + ((z // (1 << f)) % 2) * sizes[-1])
+
+    def fold_copy(f):
+        there = bases[f] + (1 - (z // (1 << f)) % 2) * sizes[f + 1]
+        rows = pl.ds(pl.multiple_of(there, sizes[f + 1]), sizes[f + 1])
         return copy_to(
-            ws.at[level], w_in.at[level], w_send.at[level], w_recv.at[level], w_peers[level], c
-        )
-
-    ws[0] = jnp.dot(
+            ws.at[rows], w_in.at[f, pl.ds(0, sizes[f + 1])], w_send.at[f], w_recv.at[f], dev_fold[f], c
+        )
+
+    def cross_copy(i):
+        return copy_to(
+            w_cross.at[i], w_cross_in.at[i], w_send.at[folds + i], w_recv.at[folds + i],
+            (dev_a, dev_b)[i], c,
+        )
+
+    def unfold_copy(f):
+        rows = pl.ds(pl.multiple_of(bases[f + 1], sizes[f + 1]), sizes[f + 1])
+        return copy_to(
+            w_full.at[c, rows], w_full.at[c, rows], w_send.at[folds + 2 + f], w_recv.at[folds + 2 + f],
+            dev_fold[f], c,
+        )
+
+    def weight_step(s):
+        if s < folds:
+            fold_copy(s).wait_recv()
+            rows = pl.ds(pl.multiple_of(bases[s + 1], sizes[s + 1]), sizes[s + 1])
+            ws[rows, :] += w_in[s, pl.ds(0, sizes[s + 1])]
+            if s + 1 < folds:
+                fold_copy(s + 1).start()
+            else:
+                w_cross[0] = ws[rows, :]
+                cross_copy(0).start()
+        elif s < folds + 2:
+            i = s - folds
+            cross_copy(i).wait_recv()
+            if i == 0:
+                w_cross[1] = w_cross[0] + w_cross_in[0]
+                cross_copy(1).start()
+            else:
+                rows = pl.ds(pl.multiple_of(bases[folds], sizes[folds]), sizes[folds])
+                w_full[c, rows] = w_cross[1] + w_cross_in[1]
+                unfold_copy(folds - 1).start()
+        else:
+            f = 2 * folds + 1 - s
+            unfold_copy(f).wait_recv()
+            if f > 0:
+                unfold_copy(f - 1).start()
+
+    weight_steps = 2 * folds + 2
+
+    ws[...] = jnp.dot(
         st[pl.ds(pl.multiple_of(c * quarter, quarter), quarter), :], ax[...],
         preferred_element_type=F32,
     )
@@ -355,7 +397,7 @@
                 ).astype(BF16)
             p_copy(j).start()
 
-            @pl.when(b_ != b)
+            @pl.when(jnp.logical_and(b_ != b, k < 8))
             def _():
                 b_copy(z_, a_).start()
 
@@ -370,14 +412,14 @@
         def _():
             copy_to(ps.at[j, c], ps.at[j, c], p_send_p.at[j], p_recv_p.at[j], d, other).wait_recv()
 
-            @pl.when(b_ != b)
+            @pl.when(jnp.logical_and(b_ != b, k < 8))
             def _():
                 b_copy(z_, a_).start()
 
         return carry
 
     lax.fori_loop(0, domains, relay_partner, 0)
-    w_copy(0).start()
+    fold_copy(0).start()
 
     def stage_a(t):
         z_ = target_layer(t)
@@ -432,21 +474,20 @@
     for r in range(2):
         part_copy(r).wait_send()
 
-    stages = max(layers + 2, levels)
+    stages = max(layers + 2, weight_steps)
     for t in range(stages):
         if t < layers:
             stage_a(t)
+        if t + 2 < layers:
+            b_copy(target_layer(t + 2), 1 - a).start()
+            b_copy(target_layer(t + 2), a).start()
         if 1 <= t <= layers:
             stage_z(t - 1)
         if 2 <= t <= layers + 1:
             stage_relay(t - 2)
-        if t < levels:
-            w_copy(t).wait_recv()
-            ws[t + 1] = ws[t] + w_in[t]
-            if t + 1 < levels:
-                w_copy(t + 1).start()
-
-    w_full[c] = ws[levels]
+        if t < weight_steps:
+            weight_step(t)
+
     w_last = copy_to(w_full.at[c], w_full.at[c], last_send.at[0], last_recv.at[0], d, other)
     w_last.start()
 
@@ -510,8 +551,11 @@
         return carry
 
     lax.fori_loop(0, layers, drain, 0)
-    for level in range(levels):
-        w_copy(level).wait_send()
+    for f in range(folds):
+        fold_copy(f).wait_send()
+        unfold_copy(f).wait_send()
+    for i in range(2):
+        cross_copy(i).wait_send()
     copy_to(fg_half.at[other], fg_half.at[other], last_send.at[1], last_recv.at[1], d, other).wait_recv()
     for h in range(2):
         fg_ref[pl.ds(h * half, half), :] = fg_half[h]
@@ -522,7 +566,7 @@
 def kernel_shards(features, weight, grad_out, tiles, tile_mask):
     domains = lax.axis_size("dom")
     layers = domains // 4
-    levels = 2 + layers.bit_length() - 1
+    folds = layers.bit_length() - 1
     sections = tiles.shape[1]
     rows, hidden = features.shape
     half, quarter = rows // 2, hidden // 2
@@ -535,7 +579,7 @@
             jax.ShapeDtypeStruct((rows, hidden), BF16),
             jax.ShapeDtypeStruct((hidden, hidden), F32),
         ),
-        in_specs=[pl.BlockSpec(memory_space=pl.ANY)] * 4 + [pl.BlockSpec(memory_space=pltpu.SMEM)],
+        in_specs=[pl.BlockSpec(memory_space=pltpu.HBM)] * 4 + [pl.BlockSpec(memory_space=pltpu.SMEM)],
         out_specs=(vmem, vmem, vmem),
         scratch_shapes=[
             pltpu.VMEM(weight.shape, BF16),
@@ -550,8 +594,10 @@
             pltpu.VMEM((2, half, hidden), F32),
             pltpu.VMEM((rows, hidden), BF16),
             pltpu.VMEM((hidden, rows), BF16),
-            pltpu.VMEM((levels + 1, quarter, hidden), F32),
-            pltpu.VMEM((levels, quarter, hidden), F32),
+            pltpu.VMEM((quarter, hidden), F32),
+            pltpu.VMEM((folds, quarter // 2, hidden), F32),
+            pltpu.VMEM((2, quarter // layers, hidden), F32),
+            pltpu.VMEM((2, quarter // layers, hidden), F32),
             pltpu.VMEM((2, quarter, hidden), F32),
             pltpu.VMEM((2, half, hidden), BF16),
             dma((2,)), dma((3,)),
@@ -562,11 +608,11 @@
             dma((layers, 2)), dma((layers, 2)),
             dma((layers,)), dma((layers,)),
             dma((layers,)), dma((2, layers)),
-            dma((levels,)), dma((levels,)),
+            dma((2 * folds + 2,)), dma((2 * folds + 2,)),
             dma((2,)), dma((2,)),
         ],
         compiler_params=pltpu.CompilerParams(
-            collective_id=0, has_side_effects=True, vmem_limit_bytes=63 * 1024 * 1024
+            collective_id=0, has_side_effects=True, vmem_limit_bytes=48 * 1024 * 1024
         ),
         cost_estimate=pl.CostEstimate(
             flops=4 * sections * rows * rows * hidden,

time: 81.8 us -> 76.9 us (0.940)
  the two profiles are of different devices: /device:TPU:1 before, /device:TPU:23 now
where the time goes in v3:
time: 76.9 us; the launch traced here: 76.7 us
  Pallas kernels  68.3 us (89%)
  local copies, waits for them, and re-layouts  7.75 us (10%)
    pallas_call x1, Pallas kernels, kernel_shards(): pl.pallas_call(functools.partial(layer_kernel, domains, float((rows * dom...  68.3 us
    unnamed x13, local copies, waits for them, and re-layouts  7.75 us

profile of v3, /device:TPU:23, one launch (start us, length us, event | category | flops | bytes accessed | tf_op | source)
XLA Modules:
  0.0 76.7 jit_solution(806648309572932024)
XLA Ops:
  0.6 0.0 copy-start
  0.6 2.2 %copy-done = bf16[1,8,512,512]{3,2,1,0:T(8,128)(2,1)S(1)} copy-done((bf16[1,8,512,512]{3,2,1,0:T(8,128)(2,1)S(1)}, bf16[1,8,512,512]{3,2,1,0:T(8,128)(2,1)}, u32[]{:S(2)}) %copy-start) | copy-done | bytes 4194328
  2.8 0.0 copy-start.1
  2.8 0.9 %copy-done.1 = bf16[512,256]{1,0:T(8,128)(2,1)S(1)} copy-done((bf16[512,256]{1,0:T(8,128)(2,1)S(1)}, bf16[512,256]{1,0:T(8,128)(2,1)}, u32[]{:S(2)}) %copy-start.1) | copy-done | bytes 262168
  3.8 0.0 copy-start.2
  3.8 0.9 %copy-done.2 = bf16[512,256]{1,0:T(8,128)(2,1)S(1)} copy-done((bf16[512,256]{1,0:T(8,128)(2,1)S(1)}, bf16[512,256]{1,0:T(8,128)(2,1)}, u32[]{:S(2)}) %copy-start.2) | copy-done | bytes 262168
  4.7 0.0 copy-start.3
  4.7 0.9 %copy-done.3 = bf16[256,256]{1,0:T(8,128)(2,1)S(1)} copy-done((bf16[256,256]{1,0:T(8,128)(2,1)S(1)}, bf16[256,256]{1,0:T(8,128)(2,1)}, u32[]{:S(2)}) %copy-start.3) | copy-done | bytes 131096
  5.6 0.0 copy-start.4
  5.6 0.7 copy-done.4
  6.3 68.3 %shard_map.76 = (bf16[512,256]{1,0:T(8,128)(2,1)S(1)}, bf16[512,256]{1,0:T(8,128)(2,1)S(1)}, f32[256,256]{1,0:T(8,128)S(1)}) custom-call(bf16[512,256]{1,0:T(8,128)(2,1)S(1)} %copy-done.1, bf16[256,256]{1,0:T(8,128)(2,1)S(1)} %copy-done.3, bf16[512,256]{1,0:T(8,128)(2,1)S(1)} %copy-done.2, bf16[1,8,512,512]{3,2,1,0:T(8,128)(2,1)S(1)} %copy-done, ...), custom_call_target="tpu_custom_call" | custom-call | flops 2147483648 | bytes 4194304 | tf_op jit(solution)/shard_map/pallas_call | solution.py:575
  74.6 0.7 copy.11
  75.3 0.7 copy.12
  76.0 0.7 copy.13
Async XLA Ops:
  0.6 2.2 %copy-start = (bf16[1,8,512,512]{3,2,1,0:T(8,128)(2,1)S(1)}, bf16[1,8,512,512]{3,2,1,0:T(8,128)(2,1)}, u32[]{:S(2)}) copy-start(bf16[1,8,512,512]{3,2,1,0:T(8,128)(2,1)} %tiles_hbm.1) | copy-start | bytes 12582916
  2.8 0.9 %copy-start.1 = (bf16[512,256]{1,0:T(8,128)(2,1)S(1)}, bf16[512,256]{1,0:T(8,128)(2,1)}, u32[]{:S(2)}) copy-start(bf16[512,256]{1,0:T(8,128)(2,1)} %x_hbm.1) | copy-start | bytes 786436
  3.8 0.9 %copy-start.2 = (bf16[512,256]{1,0:T(8,128)(2,1)S(1)}, bf16[512,256]{1,0:T(8,128)(2,1)}, u32[]{:S(2)}) copy-start(bf16[512,256]{1,0:T(8,128)(2,1)} %g_hbm.1) | copy-start | bytes 786436
  4.7 0.9 %copy-start.3 = (bf16[256,256]{1,0:T(8,128)(2,1)S(1)}, bf16[256,256]{1,0:T(8,128)(2,1)}, u32[]{:S(2)}) copy-start(bf16[256,256]{1,0:T(8,128)(2,1)} %w_hbm.1) | copy-start | bytes 393220
  5.6 0.7 copy-start.4

commit v4 on v3

--- a/solution.py
+++ b/solution.py
@@ -83,9 +83,9 @@
 def layer_kernel(
     domains, scaling,
     x_hbm, w_hbm, g_hbm, tiles_hbm, mask_ref,
-    act_ref, fg_ref, wg_ref,
-    w_ref, g_ref, tiles, xs, ps, from_b, from_a, from_z, part, part_in, ax, st, ws, w_in, w_cross, w_cross_in, w_full, fg_half,
-    own_sem, tile_sem, x_recv, x_recv_p, x_send_z, x_send_a, x_send_b, x_send_p,
+    act_hbm, fg_hbm, wg_hbm,
+    act_ref, wg_ref, w_ref, g_ref, tiles, xs, ps, from_b, from_a, from_z, part, part_in, ax, st, ws, w_in, w_cross, w_cross_in, w_full, fg_half,
+    own_sem, tile_sem, out_sem, x_recv, x_recv_p, x_send_z, x_send_a, x_send_b, x_send_p,
     part_send, part_recv,
     p_recv_p, p_send_p, b_send, b_recv, a_send, a_recv, z_send, z_recv,
     w_send, w_recv, last_send, last_recv,
@@ -294,6 +294,8 @@
         act_ref[rows, :] = (total * gate).astype(BF16)
         score = g_ref[rows, :].astype(F32) * gate * (1.0 + total * (1.0 - gate))
         st[:, rows] = jnp.transpose(score).astype(BF16)
+    act_out = pltpu.make_async_copy(act_ref, act_hbm, out_sem.at[0])
+    act_out.start()
 
     quarter = hidden // 2
     sizes, bases = [quarter], [0]
@@ -353,9 +355,17 @@
         st[pl.ds(pl.multiple_of(c * quarter, quarter), quarter), :], ax[...],
         preferred_element_type=F32,
     )
+    fold_copy(0).start()
+
+    near = jnp.minimum(z, layers - 1 - z)
+    reach = layers - 1 - near
+    long_side = jnp.where(z == near, 1, -1)
 
     def target_layer(t):
-        return jnp.where(t % 2 == 0, layers - 1 - t // 2, t // 2)
+        u = t - (reach - near)
+        return jnp.where(
+            u < 0, z + long_side * (reach - t), z + (1 - 2 * (u % 2)) * (near - u // 2)
+        )
 
     def piece(k):
         z_ = target_layer(k // 4)
@@ -419,7 +429,6 @@
         return carry
 
     lax.fori_loop(0, domains, relay_partner, 0)
-    fold_copy(0).start()
 
     def stage_a(t):
         z_ = target_layer(t)
@@ -474,19 +483,23 @@
     for r in range(2):
         part_copy(r).wait_send()
 
-    stages = max(layers + 2, weight_steps)
+    stages = max(layers + 1, (weight_steps + 1) // 2)
     for t in range(stages):
         if t < layers:
             stage_a(t)
+        if 2 * t < weight_steps:
+            weight_step(2 * t)
         if t + 2 < layers:
             b_copy(target_layer(t + 2), 1 - a).start()
             b_copy(target_layer(t + 2), a).start()
         if 1 <= t <= layers:
             stage_z(t - 1)
-        if 2 <= t <= layers + 1:
-            stage_relay(t - 2)
-        if t < weight_steps:
-            weight_step(t)
+        if t == 2:
+            stage_relay(0)
+        if 2 <= t <= layers:
+            stage_relay(t - 1)
+        if 2 * t + 1 < weight_steps:
+            weight_step(2 * t + 1)
 
     w_last = copy_to(w_full.at[c], w_full.at[c], last_send.at[0], last_recv.at[0], d, other)
     w_last.start()
@@ -508,9 +521,18 @@
     f_last = copy_to(fg_half.at[c], fg_half.at[c], last_send.at[1], last_recv.at[1], d, other)
     f_last.start()
 
+    def fg_out(h):
+        return pltpu.make_async_copy(
+            fg_half.at[h], fg_hbm.at[pl.ds(pl.multiple_of(h * half, half), half)], out_sem.at[1 + h]
+        )
+
+    fg_out(c).start()
+
     copy_to(w_full.at[other], w_full.at[other], last_send.at[0], last_recv.at[0], d, other).wait_recv()
     for h in range(2):
         wg_ref[:, pl.ds(h * quarter, quarter)] = jnp.transpose(w_full[h]) * scaling
+    wg_out = pltpu.make_async_copy(wg_ref, wg_hbm, out_sem.at[3])
+    wg_out.start()
 
     def drain_p(j, carry):
         @pl.when(jnp.logical_and(owner(j) != c, j != d))
@@ -557,10 +579,26 @@
     for i in range(2):
         cross_copy(i).wait_send()
     copy_to(fg_half.at[other], fg_half.at[other], last_send.at[1], last_recv.at[1], d, other).wait_recv()
-    for h in range(2):
-        fg_ref[pl.ds(h * half, half), :] = fg_half[h]
+    fg_out(other).start()
     w_last.wait_send()
     f_last.wait_send()
+    act_out.wait()
+    wg_out.wait()
+    for h in range(2):
+        fg_out(h).wait()
+
+
+def finish_kernel(act, fg, wg, act_out, fg_out, wg_out, sem):
+    copies = []
+    for src, dst in ((act, act_out), (fg, fg_out), (wg, wg_out)):
+        rows = src.shape[0] // 2
+        for h in range(2):
+            part = pl.ds(h * rows, rows)
+            copies.append(pltpu.make_async_copy(src.at[part], dst.at[part], sem.at[len(copies)]))
+    for copy in copies:
+        copy.start()
+    for copy in copies:
+        copy.wait()
 
 
 def kernel_shards(features, weight, grad_out, tiles, tile_mask):
@@ -571,17 +609,20 @@
     rows, hidden = features.shape
     half, quarter = rows // 2, hidden // 2
     dma = pltpu.SemaphoreType.DMA
-    vmem = pl.BlockSpec(memory_space=pltpu.VMEM)
-    return pl.pallas_call(
+    out_shape = (
+        jax.ShapeDtypeStruct((rows, hidden), BF16),
+        jax.ShapeDtypeStruct((rows, hidden), BF16),
+        jax.ShapeDtypeStruct((hidden, hidden), F32),
+    )
+    anywhere = [pl.BlockSpec(memory_space=pl.ANY)] * 3
+    results = pl.pallas_call(
         functools.partial(layer_kernel, domains, float((rows * domains) ** (-0.5))),
-        out_shape=(
-            jax.ShapeDtypeStruct((rows, hidden), BF16),
-            jax.ShapeDtypeStruct((rows, hidden), BF16),
-            jax.ShapeDtypeStruct((hidden, hidden), F32),
-        ),
+        out_shape=out_shape,
         in_specs=[pl.BlockSpec(memory_space=pltpu.HBM)] * 4 + [pl.BlockSpec(memory_space=pltpu.SMEM)],
-        out_specs=(vmem, vmem, vmem),
+        out_specs=anywhere,
         scratch_shapes=[
+            pltpu.VMEM((rows, hidden), BF16),
+            pltpu.VMEM((hidden, hidden), F32),
             pltpu.VMEM(weight.shape, BF16),
             pltpu.VMEM((rows, hidden), BF16),
             pltpu.VMEM(tiles.shape[1:], BF16),
@@ -600,7 +641,7 @@
             pltpu.VMEM((2, quarter // layers, hidden), F32),
             pltpu.VMEM((2, quarter, hidden), F32),
             pltpu.VMEM((2, half, hidden), BF16),
-            dma((2,)), dma((3,)),
+            dma((2,)), dma((3,)), dma((4,)),
             dma((domains,)), dma((domains,)),
             dma((2, layers)), dma((layers,)), dma((layers, 2)), dma((domains,)),
             dma((2,)), dma((2,)),
@@ -612,7 +653,7 @@
             dma((2,)), dma((2,)),
         ],
         compiler_params=pltpu.CompilerParams(
-            collective_id=0, has_side_effects=True, vmem_limit_bytes=48 * 1024 * 1024
+            collective_id=0, has_side_effects=True, vmem_limit_bytes=63 * 1024 * 1024
         ),
         cost_estimate=pl.CostEstimate(
             flops=4 * sections * rows * rows * hidden,
@@ -620,6 +661,14 @@
             transcendentals=rows * hidden,
         ),
     )(features, weight, grad_out, tiles, tile_mask)
+    return pl.pallas_call(
+        finish_kernel,
+        out_shape=out_shape,
+        in_specs=anywhere,
+        out_specs=anywhere,
+        scratch_shapes=[dma((6,))],
+        cost_estimate=pl.CostEstimate(flops=0, bytes_accessed=6 * rows * hidden * 2, transcendentals=0),
+    )(*results)
 
 
 def solution(mesh):

time: 76.9 us -> 91.7 us (1.19)
  the two profiles are of different devices: /device:TPU:23 before, /device:TPU:1 now
where the time goes in v4:
time: 91.7 us; the launch traced here: 91.6 us
  Pallas kernels  90.9 us (99%)
    pallas_call x1, Pallas kernels, kernel_shards(): pl.pallas_call(functools.partial(layer_kernel, domains, float((rows * dom...  65.9 us
    pallas_call x1, Pallas kernels, kernel_shards(): pl.pallas_call(finish_kernel, out_shape=out_shape, in_specs=anywhere, out...  25 us

profile of v4, /device:TPU:1, one launch (start us, length us, event | category | flops | bytes accessed | tf_op | source)
XLA Modules:
  0.0 91.6 jit_solution(7020602188611793573)
XLA Ops:
  0.6 65.9 %shard_map.76 = (bf16[512,256]{1,0:T(8,128)(2,1)}, bf16[512,256]{1,0:T(8,128)(2,1)}, f32[256,256]{1,0:T(8,128)}) custom-call(bf16[512,256]{1,0:T(8,128)(2,1)} %x_hbm.1, bf16[256,256]{1,0:T(8,128)(2,1)} %w_hbm.1, bf16[512,256]{1,0:T(8,128)(2,1)} %g_hbm.1, bf16[1,8,512,512]{3,2,1,0:T(8,128)(2,1)} %tiles_hbm.1, s32[1,8]{1,0:T(1,128)} %mask_ref.1), custom_call_target="tpu_custom_call" | custom-call | flops 2147483648 | bytes 4194304 | tf_op jit(solution)/shard_map/pallas_call | solution.py:618
  66.6 25.0 %shard_map.77 = (bf16[512,256]{1,0:T(8,128)(2,1)}, bf16[512,256]{1,0:T(8,128)(2,1)}, f32[256,256]{1,0:T(8,128)}) custom-call(bf16[512,256]{1,0:T(8,128)(2,1)} %get-tuple-element.6.act, bf16[512,256]{1,0:T(8,128)(2,1)} %get-tuple-element.7.fg, f32[256,256]{1,0:T(8,128)} %get-tuple-element.8.wg), custom_call_target="tpu_custom_call" | custom-call | bytes 1572864 | tf_op jit(solution)/shard_map/pallas_call | solution.py:664

commit v5 on v4

--- a/solution.py
+++ b/solution.py
@@ -86,6 +86,7 @@
     act_hbm, fg_hbm, wg_hbm,
     act_ref, wg_ref, w_ref, g_ref, tiles, xs, ps, from_b, from_a, from_z, part, part_in, ax, st, ws, w_in, w_cross, w_cross_in, w_full, fg_half,
     own_sem, tile_sem, out_sem, x_recv, x_recv_p, x_send_z, x_send_a, x_send_b, x_send_p,
+    y_send, y_recv, y_send_z, y_recv_z, y_send_p, y_recv_p,
     part_send, part_recv,
     p_recv_p, p_send_p, b_send, b_recv, a_send, a_recv, z_send, z_recv,
     w_send, w_recv, last_send, last_recv,
@@ -95,6 +96,8 @@
     sections = domains // 2
     half = x_hbm.shape[0] // 2
     hidden = x_hbm.shape[1]
+    cut = half * 3 // 4
+    main, rest = pl.ds(0, cut), pl.ds(cut, half - cut)
     d = lax.axis_index("dom")
     c = lax.axis_index("rep")
     other = 1 - c
@@ -147,19 +150,86 @@
         return ((d - j + domains) % domains) // sections
 
     def x_copy_z(j, z_, up):
-        return copy_to(xs.at[j, c], xs.at[j, c], x_send_z.at[up, z_], x_recv.at[j], d - 4 + 8 * up, c)
+        return copy_to(xs.at[j, c, main], xs.at[j, c, main], x_send_z.at[up, z_], x_recv.at[j], d - 4 + 8 * up, c)
 
     def x_copy_a(j, z_):
-        return copy_to(xs.at[j, c], xs.at[j, c], x_send_a.at[z_], x_recv.at[j], dev_a, c)
+        return copy_to(xs.at[j, c, main], xs.at[j, c, main], x_send_a.at[z_], x_recv.at[j], dev_a, c)
 
     def x_copy_b(j, z_, a_):
-        return copy_to(xs.at[j, c], xs.at[j, c], x_send_b.at[z_, a_], x_recv.at[j], dev_b, c)
+        return copy_to(xs.at[j, c, main], xs.at[j, c, main], x_send_b.at[z_, a_], x_recv.at[j], dev_b, c)
 
     def x_copy_p(j):
-        return copy_to(xs.at[j, c], xs.at[j, c], x_send_p.at[j], x_recv_p.at[j], d, other)
+        return copy_to(xs.at[j, c, main], xs.at[j, c, main], x_send_p.at[j], x_recv_p.at[j], d, other)
+
+    def y_copy_a():
+        return copy_to(
+            xs.at[d, c, rest], xs.at[d, c, rest], y_send.at[2], y_recv.at[d % 4], dev_a, c
+        )
+
+    def y_copy_b(a_):
+        j = block_at(z, b, a_)
+        return copy_to(xs.at[j, c, rest], xs.at[j, c, rest], y_send.at[a_], y_recv.at[j % 4], dev_b, c)
+
+    def y_slab(z_, up):
+        slab = xs.at[pl.ds(z_ * 4, 4), c, rest]
+        return copy_to(slab, slab, y_send_z.at[up, z_], y_recv_z.at[z_], d - 4 + 8 * up, c)
+
+    def y_copy_p(j):
+        return copy_to(
+            xs.at[j, c, rest], xs.at[j, c, rest], y_send_p.at[j], y_recv_p.at[j], d, other
+        )
+
+    def y_wait(b_, a_):
+        j = block_at(z, b_, a_)
+        copy_to(
+            xs.at[j, c, rest], xs.at[j, c, rest], y_send.at[2], y_recv.at[j % 4], dev_a, c
+        ).wait_recv()
+
+    def y_to_partner(z_):
+        def one(q, carry):
+            j = z_ * 4 + q
+
+            @pl.when(jnp.logical_and(owner(j) != c, j != d))
+            def _():
+                y_copy_p(j).start()
+
+            return carry
+
+        lax.fori_loop(0, 4, one, 0)
+
+    def y_layer_done():
+        y_wait(1 - b, a)
+        y_wait(1 - b, 1 - a)
+
+        @pl.when(z > 0)
+        def _():
+            y_slab(z, 0).start()
+
+        @pl.when(z < layers - 1)
+        def _():
+            y_slab(z, 1).start()
+
+        y_to_partner(z)
+
+    def y_from_layer(n):
+        z_ = layer_of(n)
+
+        @pl.when(in_range(z_))
+        def _():
+            y_slab(z_, 0).wait_recv()
+
+            @pl.when(jnp.logical_and(z_ < z, z < layers - 1))
+            def _():
+                y_slab(z_, 1).start()
+
+            @pl.when(jnp.logical_and(z_ > z, z > 0))
+            def _():
+                y_slab(z_, 0).start()
+
+            y_to_partner(z_)
 
     def x_arrive(j):
-        copy_to(xs.at[j, c], xs.at[j, c], x_send_p.at[j], x_recv.at[j], d, other).wait_recv()
+        copy_to(xs.at[j, c, main], xs.at[j, c, main], x_send_p.at[j], x_recv.at[j], d, other).wait_recv()
 
         @pl.when(owner(j) != c)
         def _():
@@ -178,6 +248,8 @@
 
     x_copy_b(d, z, a).start()
     x_copy_a(d, z).start()
+    y_copy_b(a).start()
+    y_copy_a().start()
 
     def layer_of(n):
         return z + ((n + 1) // 2) * (2 * ((n + 1) % 2) - 1)
@@ -244,9 +316,10 @@
             def _():
                 @pl.when(j != d)
                 def _():
-                    copy_to(
-                        xs.at[j, other], xs.at[j, other], x_send_p.at[j], x_recv_p.at[j], d, other
-                    ).wait_recv()
+                    for send, recv, rows in ((x_send_p, x_recv_p, main), (y_send_p, y_recv_p, rest)):
+                        copy_to(
+                            xs.at[j, other, rows], xs.at[j, other, rows], send.at[j], recv.at[j], d, other
+                        ).wait_recv()
 
                 product(j)
 
@@ -262,6 +335,9 @@
     for r in range(2):
         part[r] = jnp.zeros((half, hidden), F32)
 
+    y_wait(b, 1 - a)
+    y_copy_b(1 - a).start()
+
     def gather_step(n, carry):
         for lag, step in enumerate((from_layer, from_a_side, from_b_side)):
             at = n - 2 * lag
@@ -269,6 +345,14 @@
             @pl.when(jnp.logical_and(at >= (1 if lag == 0 else 0), at < visits))
             def _():
                 step(at)
+
+        @pl.when(n == 2)
+        def _():
+            y_layer_done()
+
+        @pl.when(jnp.logical_and(n >= 4, n - 3 < visits))
+        def _():
+            y_from_layer(n - 3)
 
         @pl.when(n >= 5)
         def _():
@@ -538,6 +622,7 @@
         @pl.when(jnp.logical_and(owner(j) != c, j != d))
         def _():
             x_copy_p(j).wait_send()
+            y_copy_p(j).wait_send()
 
         @pl.when(owner(j) == c)
         def _():
@@ -551,10 +636,12 @@
         @pl.when(jnp.logical_and(z_ <= z, z < layers - 1))
         def _():
             x_copy_z(block_at(z_, b, a), z_, 1).wait_send()
+            y_slab(z_, 1).wait_send()
 
         @pl.when(jnp.logical_and(z_ >= z, z > 0))
         def _():
             x_copy_z(block_at(z_, b, a), z_, 0).wait_send()
+            y_slab(z_, 0).wait_send()
 
         x_copy_a(block_at(z_, b, a), z_).wait_send()
         a_copy(z_).wait_send()
@@ -573,6 +660,9 @@
         return carry
 
     lax.fori_loop(0, layers, drain, 0)
+    y_copy_a().wait_send()
+    for a_ in range(2):
+        y_copy_b(a_).wait_send()
     for f in range(folds):
         fold_copy(f).wait_send()
         unfold_copy(f).wait_send()
@@ -588,16 +678,16 @@
         fg_out(h).wait()
 
 
-def finish_kernel(act, fg, wg, act_out, fg_out, wg_out, sem):
-    copies = []
-    for src, dst in ((act, act_out), (fg, fg_out), (wg, wg_out)):
-        rows = src.shape[0] // 2
-        for h in range(2):
-            part = pl.ds(h * rows, rows)
-            copies.append(pltpu.make_async_copy(src.at[part], dst.at[part], sem.at[len(copies)]))
-    for copy in copies:
+def finish_kernel(act, fg, wg, act_out, fg_out, wg_out, act_v, fg_v, wg_v, sem):
+    pairs = ((act, act_v, act_out), (fg, fg_v, fg_out), (wg, wg_v, wg_out))
+    inward = [pltpu.make_async_copy(p[0], p[1], sem.at[0, i]) for i, p in enumerate(pairs)]
+    outward = [pltpu.make_async_copy(p[1], p[2], sem.at[1, i]) for i, p in enumerate(pairs)]
+    for copy in inward:
         copy.start()
-    for copy in copies:
+    for first, second in zip(inward, outward):
+        first.wait()
+        second.start()
+    for copy in outward:
         copy.wait()
 
 
@@ -644,6 +734,7 @@
             dma((2,)), dma((3,)), dma((4,)),
             dma((domains,)), dma((domains,)),
             dma((2, layers)), dma((layers,)), dma((layers, 2)), dma((domains,)),
+            dma((3,)), dma((4,)), dma((2, layers)), dma((layers,)), dma((domains,)), dma((domains,)),
             dma((2,)), dma((2,)),
             dma((domains,)), dma((domains,)),
             dma((layers, 2)), dma((layers, 2)),
@@ -666,7 +757,13 @@
         out_shape=out_shape,
         in_specs=anywhere,
         out_specs=anywhere,
-        scratch_shapes=[dma((6,))],
+        scratch_shapes=[
+            pltpu.VMEM((rows, hidden), BF16),
+            pltpu.VMEM((rows, hidden), BF16),
+            pltpu.VMEM((hidden, hidden), F32),
+            dma((2, 3)),
+        ],
+        compiler_params=pltpu.CompilerParams(vmem_limit_bytes=63 * 1024 * 1024),
         cost_estimate=pl.CostEstimate(flops=0, bytes_accessed=6 * rows * hidden * 2, transcendentals=0),
     )(*results)
 

time: 91.7 us -> 67.9 us (0.74)
  Pallas kernels: 90.9 us -> 66.6 us
    pallas_call x1, Pallas kernels: 25 us -> 1.88 us  [kernel_shards(): pl.pallas_call(finish_kernel, out_shape=out_shape, in_specs=anywhere, out...]
    pallas_call x1, Pallas kernels: 65.9 us -> 64.7 us  [kernel_shards(): pl.pallas_call(functools.partial(layer_kernel, domains, float((rows * dom...]
where the time goes in v5:
time: 67.9 us; the launch traced here: 67.2 us
  Pallas kernels  66.6 us (98%)
    pallas_call x1, Pallas kernels, kernel_shards(): pl.pallas_call(functools.partial(layer_kernel, domains, float((rows * dom...  64.7 us
    pallas_call x1, Pallas kernels, kernel_shards(): pl.pallas_call(finish_kernel, out_shape=out_shape, in_specs=anywhere, out...  1.88 us

profile of v5, /device:TPU:1, one launch (start us, length us, event | category | flops | bytes accessed | tf_op | source)
XLA Modules:
  0.0 67.2 jit_solution(8979422150108137211)
XLA Ops:
  0.6 64.7 %shard_map.76 = (bf16[512,256]{1,0:T(8,128)(2,1)}, bf16[512,256]{1,0:T(8,128)(2,1)}, f32[256,256]{1,0:T(8,128)}) custom-call(bf16[512,256]{1,0:T(8,128)(2,1)} %x_hbm.1, bf16[256,256]{1,0:T(8,128)(2,1)} %w_hbm.1, bf16[512,256]{1,0:T(8,128)(2,1)} %g_hbm.1, bf16[1,8,512,512]{3,2,1,0:T(8,128)(2,1)} %tiles_hbm.1, s32[1,8]{1,0:T(1,128)} %mask_ref.1), custom_call_target="tpu_custom_call" | custom-call | flops 2147483648 | bytes 4194304 | tf_op jit(solution)/shard_map/pallas_call | solution.py:708
  65.4 1.9 %shard_map.77 = (bf16[512,256]{1,0:T(8,128)(2,1)}, bf16[512,256]{1,0:T(8,128)(2,1)}, f32[256,256]{1,0:T(8,128)}) custom-call(bf16[512,256]{1,0:T(8,128)(2,1)} %get-tuple-element.6.act, bf16[512,256]{1,0:T(8,128)(2,1)} %get-tuple-element.7.fg, f32[256,256]{1,0:T(8,128)} %get-tuple-element.8.wg), custom_call_target="tpu_custom_call" | custom-call | bytes 1572864 | tf_op jit(solution)/shard_map/pallas_call | solution.py:755

commit v6 on v5

--- a/solution.py
+++ b/solution.py
@@ -84,10 +84,11 @@
     domains, scaling,
     x_hbm, w_hbm, g_hbm, tiles_hbm, mask_ref,
     act_hbm, fg_hbm, wg_hbm,
-    act_ref, wg_ref, w_ref, g_ref, tiles, xs, ps, from_b, from_a, from_z, part, part_in, ax, st, ws, w_in, w_cross, w_cross_in, w_full, fg_half,
+    act_ref, wg_ref, w_ref, g_ref, tiles, xs, ps, rest_z, rest_in, from_b, from_a, from_z, part, part_in, ax, st, ws, w_in, w_cross, w_cross_in, w_full, fg_half,
     own_sem, tile_sem, out_sem, x_recv, x_recv_p, x_send_z, x_send_a, x_send_b, x_send_p,
     y_send, y_recv, y_send_z, y_recv_z, y_send_p, y_recv_p,
     part_send, part_recv,
+    r_send, r_recv, r_send_in, r_recv_in,
     p_recv_p, p_send_p, b_send, b_recv, a_send, a_recv, z_send, z_recv,
     w_send, w_recv, last_send, last_recv,
 ):
@@ -96,7 +97,7 @@
     sections = domains // 2
     half = x_hbm.shape[0] // 2
     hidden = x_hbm.shape[1]
-    cut = half * 3 // 4
+    cut = half * 7 // 8
     main, rest = pl.ds(0, cut), pl.ds(cut, half - cut)
     d = lax.axis_index("dom")
     c = lax.axis_index("rep")
@@ -339,7 +340,7 @@
     y_copy_b(1 - a).start()
 
     def gather_step(n, carry):
-        for lag, step in enumerate((from_layer, from_a_side, from_b_side)):
+        for lag, step in ((1, from_a_side), (0, from_layer), (2, from_b_side)):
             at = n - 2 * lag
 
             @pl.when(jnp.logical_and(at >= (1 if lag == 0 else 0), at < visits))
@@ -463,20 +464,86 @@
 
     def b_copy(z_, a_):
         return copy_to(
-            ps.at[block_at(z_, 1 - b, a_), c], from_b.at[z_, a_], b_send.at[z_, a_], b_recv.at[z_, a_],
-            dev_b, c,
+            ps.at[block_at(z_, 1 - b, a_), c, main], from_b.at[z_, a_, main],
+            b_send.at[z_, a_], b_recv.at[z_, a_], dev_b, c,
         )
 
     def a_copy(z_):
         return copy_to(
-            ps.at[block_at(z_, b, 1 - a), c], from_a.at[z_], a_send.at[z_], a_recv.at[z_], dev_a, c
+            ps.at[block_at(z_, b, 1 - a), c, main], from_a.at[z_, main],
+            a_send.at[z_], a_recv.at[z_], dev_a, c,
         )
 
     def z_copy(z_, up):
         return copy_to(
-            ps.at[block_at(z_, b, a), c], from_z.at[up, z_], z_send.at[z_], z_recv.at[up, z_],
-            d - 4 + 8 * up, c,
-        )
+            ps.at[block_at(z_, b, a), c, main], from_z.at[up, z_, main],
+            z_send.at[z_], z_recv.at[up, z_], d - 4 + 8 * up, c,
+        )
+
+    def r_slab(z_, up):
+        return copy_to(
+            ps.at[pl.ds(z_ * 4, 4), c, rest], rest_z.at[up, z_],
+            r_send.at[z_], r_recv.at[up, z_], d - 4 + 8 * up, c,
+        )
+
+    def r_copy_b(a_):
+        return copy_to(
+            ps.at[block_at(z, 1 - b, a_), c, rest], rest_in.at[a_],
+            r_send_in.at[a_], r_recv_in.at[a_], dev_b, c,
+        )
+
+    def r_copy_a():
+        return copy_to(
+            ps.at[block_at(z, b, 1 - a), c, rest], rest_in.at[2],
+            r_send_in.at[2], r_recv_in.at[2], dev_a, c,
+        )
+
+    def rest_add(z_, up):
+        r_slab(z_, up).wait_recv()
+        slab = pl.ds(z_ * 4, 4)
+        ps[slab, c, rest] = (ps[slab, c, rest].astype(F32) + rest_z[up, z_].astype(F32)).astype(BF16)
+
+    def rest_first(t):
+        z_ = target_layer(t)
+
+        @pl.when(jnp.logical_and(z_ > z, z == 0))
+        def _():
+            r_slab(z_, 1).start()
+
+        @pl.when(jnp.logical_and(z_ < z, z == layers - 1))
+        def _():
+            r_slab(z_, 0).start()
+
+    def rest_relay(t):
+        z_ = target_layer(t)
+
+        @pl.when(jnp.logical_and(z_ > z, z > 0))
+        def _():
+            rest_add(z_, 1)
+            r_slab(z_, 1).start()
+
+        @pl.when(jnp.logical_and(z_ < z, z < layers - 1))
+        def _():
+            rest_add(z_, 0)
+            r_slab(z_, 0).start()
+
+    def rest_own():
+        @pl.when(z > 0)
+        def _():
+            rest_add(z, 1)
+
+        @pl.when(z < layers - 1)
+        def _():
+            rest_add(z, 0)
+
+        r_copy_b(1 - a).start()
+        r_copy_b(a).start()
+
+    def rest_round():
+        r_copy_b(1 - a).wait_recv()
+        j = block_at(z, b, 1 - a)
+        ps[j, c, rest] = (ps[j, c, rest].astype(F32) + rest_in[1 - a].astype(F32)).astype(BF16)
+        r_copy_a().start()
 
     def backward(k, carry):
         z_, b_, a_, j = piece(k)
@@ -518,7 +585,9 @@
         z_ = target_layer(t)
         b_copy(z_, 1 - a).wait_recv()
         j = block_at(z_, b, 1 - a)
-        ps[j, c] = (ps[j, c].astype(F32) + from_b[z_, 1 - a].astype(F32)).astype(BF16)
+        ps[j, c, main] = (
+            ps[j, c, main].astype(F32) + from_b[z_, 1 - a, main].astype(F32)
+        ).astype(BF16)
         a_copy(z_).start()
 
     def stage_z(t):
@@ -528,20 +597,23 @@
         j = block_at(z_, b, a)
 
         def mine():
-            return ps[j, c].astype(F32) + from_b[z_, a].astype(F32) + from_a[z_].astype(F32)
+            return (
+                ps[j, c, main].astype(F32) + from_b[z_, a, main].astype(F32)
+                + from_a[z_, main].astype(F32)
+            )
 
         @pl.when(z_ == z)
         def _():
-            part[0] = mine()
+            part[0, main] = mine()
 
         @pl.when(jnp.logical_and(z_ > z, z == 0))
         def _():
-            ps[j, c] = mine().astype(BF16)
+            ps[j, c, main] = mine().astype(BF16)
             z_copy(z_, 1).start()
 
         @pl.when(jnp.logical_and(z_ < z, z == layers - 1))
         def _():
-            ps[j, c] = mine().astype(BF16)
+            ps[j, c, main] = mine().astype(BF16)
             z_copy(z_, 0).start()
 
     def stage_relay(t):
@@ -550,9 +622,9 @@
 
         def pass_on(up):
             z_copy(z_, up).wait_recv()
-            ps[j, c] = (
-                ps[j, c].astype(F32) + from_b[z_, a].astype(F32) + from_a[z_].astype(F32)
-                + from_z[up, z_].astype(F32)
+            ps[j, c, main] = (
+                ps[j, c, main].astype(F32) + from_b[z_, a, main].astype(F32)
+                + from_a[z_, main].astype(F32) + from_z[up, z_, main].astype(F32)
             ).astype(BF16)
             z_copy(z_, up).start()
 
@@ -566,6 +638,9 @@
 
     for r in range(2):
         part_copy(r).wait_send()
+
+    for t in range(layers - 1):
+        rest_first(t)
 
     stages = max(layers + 1, (weight_steps + 1) // 2)
     for t in range(stages):
@@ -582,6 +657,12 @@
             stage_relay(0)
         if 2 <= t <= layers:
             stage_relay(t - 1)
+        if 1 <= t < layers:
+            rest_relay(t - 1)
+        if t == layers - 1:
+            rest_own()
+        if t == layers:
+            rest_round()
         if 2 * t + 1 < weight_steps:
             weight_step(2 * t + 1)
 
@@ -591,13 +672,18 @@
     @pl.when(z > 0)
     def _():
         z_copy(z, 1).wait_recv()
-        part[0] += from_z[1, z].astype(F32)
+        part[0, main] += from_z[1, z, main].astype(F32)
 
     @pl.when(z < layers - 1)
     def _():
         z_copy(z, 0).wait_recv()
-        part[0] += from_z[0, z].astype(F32)
-
+        part[0, main] += from_z[0, z, main].astype(F32)
+
+    r_copy_b(a).wait_recv()
+    r_copy_a().wait_recv()
+    part[0, rest] = (
+        ps[d, c, rest].astype(F32) + rest_in[a].astype(F32) + rest_in[2].astype(F32)
+    )
     node = jnp.transpose(part[0]).astype(BF16)
     fg_half[c] = lax.dot_general(
         node, w_ref[...], (((1,), (1,)), ((), ())), preferred_element_type=F32
@@ -652,10 +738,12 @@
         @pl.when(z_ > z)
         def _():
             z_copy(z_, 1).wait_send()
+            r_slab(z_, 1).wait_send()
 
         @pl.when(z_ < z)
         def _():
             z_copy(z_, 0).wait_send()
+            r_slab(z_, 0).wait_send()
 
         return carry
 
@@ -663,6 +751,8 @@
     y_copy_a().wait_send()
     for a_ in range(2):
         y_copy_b(a_).wait_send()
+        r_copy_b(a_).wait_send()
+    r_copy_a().wait_send()
     for f in range(folds):
         fold_copy(f).wait_send()
         unfold_copy(f).wait_send()
@@ -718,6 +808,8 @@
             pltpu.VMEM(tiles.shape[1:], BF16),
             pltpu.VMEM((domains, 2, half, hidden), BF16),
             pltpu.VMEM((domains, 2, hidden, half), BF16),
+            pltpu.VMEM((2, layers, 4, half // 8, half), BF16),
+            pltpu.VMEM((3, half // 8, half), BF16),
             pltpu.VMEM((layers, 2, hidden, half), BF16),
             pltpu.VMEM((layers, hidden, half), BF16),
             pltpu.VMEM((2, layers, hidden, half), BF16),
@@ -736,6 +828,7 @@
             dma((2, layers)), dma((layers,)), dma((layers, 2)), dma((domains,)),
             dma((3,)), dma((4,)), dma((2, layers)), dma((layers,)), dma((domains,)), dma((domains,)),
             dma((2,)), dma((2,)),
+            dma((layers,)), dma((2, layers)), dma((3,)), dma((3,)),
             dma((domains,)), dma((domains,)),
             dma((layers, 2)), dma((layers, 2)),
             dma((layers,)), dma((layers,)),

time: 67.9 us -> 74.8 us (1.10)
  Pallas kernels: 66.6 us -> 74 us
    pallas_call x1, Pallas kernels: 64.7 us -> 72.2 us  [kernel_shards(): pl.pallas_call(functools.partial(layer_kernel, domains, float((rows * dom...]
where the time goes in v6:
time: 74.8 us; the launch traced here: 74.7 us
  Pallas kernels  74 us (99%)
    pallas_call x1, Pallas kernels, kernel_shards(): pl.pallas_call(functools.partial(layer_kernel, domains, float((rows * dom...  72.2 us
    pallas_call x1, Pallas kernels, kernel_shards(): pl.pallas_call(finish_kernel, out_shape=out_shape, in_specs=anywhere, out...  1.88 us

profile of v6, /device:TPU:1, one launch (start us, length us, event | category | flops | bytes accessed | tf_op | source)
XLA Modules:
  0.0 74.7 jit_solution(2034062104955484901)
XLA Ops:
  0.6 72.2 %shard_map.76 = (bf16[512,256]{1,0:T(8,128)(2,1)}, bf16[512,256]{1,0:T(8,128)(2,1)}, f32[256,256]{1,0:T(8,128)}) custom-call(bf16[512,256]{1,0:T(8,128)(2,1)} %x_hbm.1, bf16[256,256]{1,0:T(8,128)(2,1)} %w_hbm.1, bf16[512,256]{1,0:T(8,128)(2,1)} %g_hbm.1, bf16[1,8,512,512]{3,2,1,0:T(8,128)(2,1)} %tiles_hbm.1, s32[1,8]{1,0:T(1,128)} %mask_ref.1), custom_call_target="tpu_custom_call" | custom-call | flops 2147483648 | bytes 4194304 | tf_op jit(solution)/shard_map/pallas_call | solution.py:798
  72.8 1.9 %shard_map.77 = (bf16[512,256]{1,0:T(8,128)(2,1)}, bf16[512,256]{1,0:T(8,128)(2,1)}, f32[256,256]{1,0:T(8,128)}) custom-call(bf16[512,256]{1,0:T(8,128)(2,1)} %get-tuple-element.6.act, bf16[512,256]{1,0:T(8,128)(2,1)} %get-tuple-element.7.fg, f32[256,256]{1,0:T(8,128)} %get-tuple-element.8.wg), custom_call_target="tpu_custom_call" | custom-call | bytes 1572864 | tf_op jit(solution)/shard_map/pallas_call | solution.py:848

commit v7 on v5

--- a/solution.py
+++ b/solution.py
@@ -96,7 +96,7 @@
     sections = domains // 2
     half = x_hbm.shape[0] // 2
     hidden = x_hbm.shape[1]
-    cut = half * 3 // 4
+    cut = half * 7 // 8
     main, rest = pl.ds(0, cut), pl.ds(cut, half - cut)
     d = lax.axis_index("dom")
     c = lax.axis_index("rep")
@@ -339,7 +339,7 @@
     y_copy_b(1 - a).start()
 
     def gather_step(n, carry):
-        for lag, step in enumerate((from_layer, from_a_side, from_b_side)):
+        for lag, step in ((1, from_a_side), (0, from_layer), (2, from_b_side)):
             at = n - 2 * lag
 
             @pl.when(jnp.logical_and(at >= (1 if lag == 0 else 0), at < visits))
@@ -478,7 +478,7 @@
             d - 4 + 8 * up, c,
         )
 
-    def backward(k, carry):
+    def backward(k):
         z_, b_, a_, j = piece(k)
 
         @pl.when(owner(j) == c)
@@ -495,24 +495,29 @@
             def _():
                 b_copy(z_, a_).start()
 
+    def relay_partner(k):
+        z_, b_, a_, j = piece(k)
+
+        @pl.when(owner(j) != c)
+        def _():
+            copy_to(ps.at[j, c], ps.at[j, c], p_send_p.at[j], p_recv_p.at[j], d, other).wait_recv()
+
+            @pl.when(jnp.logical_and(b_ != b, k < 8))
+            def _():
+                b_copy(z_, a_).start()
+
+    def backward_step(k, carry):
+        @pl.when(k < domains)
+        def _():
+            backward(k)
+
+        @pl.when(k >= 4)
+        def _():
+            relay_partner(k - 4)
+
         return carry
 
-    lax.fori_loop(0, domains, backward, 0)
-
-    def relay_partner(k, carry):
-        z_, b_, a_, j = piece(k)
-
-        @pl.when(owner(j) != c)
-        def _():
-            copy_to(ps.at[j, c], ps.at[j, c], p_send_p.at[j], p_recv_p.at[j], d, other).wait_recv()
-
-            @pl.when(jnp.logical_and(b_ != b, k < 8))
-            def _():
-                b_copy(z_, a_).start()
-
-        return carry
-
-    lax.fori_loop(0, domains, relay_partner, 0)
+    lax.fori_loop(0, domains + 4, backward_step, 0)
 
     def stage_a(t):
         z_ = target_layer(t)

time: 67.9 us -> 67.4 us (level)
  no operation moved by 1% of the time
where the time goes in v7:
time: 67.4 us; the launch traced here: 67.2 us
  Pallas kernels  66.6 us (99%)
    pallas_call x1, Pallas kernels, kernel_shards(): pl.pallas_call(functools.partial(layer_kernel, domains, float((rows * dom...  64.7 us
    pallas_call x1, Pallas kernels, kernel_shards(): pl.pallas_call(finish_kernel, out_shape=out_shape, in_specs=anywhere, out...  1.88 us

profile of v7, /device:TPU:1, one launch (start us, length us, event | category | flops | bytes accessed | tf_op | source)
XLA Modules:
  0.0 67.2 jit_solution(6181223050261863757)
XLA Ops:
  0.6 64.7 %shard_map.76 = (bf16[512,256]{1,0:T(8,128)(2,1)}, bf16[512,256]{1,0:T(8,128)(2,1)}, f32[256,256]{1,0:T(8,128)}) custom-call(bf16[512,256]{1,0:T(8,128)(2,1)} %x_hbm.1, bf16[256,256]{1,0:T(8,128)(2,1)} %w_hbm.1, bf16[512,256]{1,0:T(8,128)(2,1)} %g_hbm.1, bf16[1,8,512,512]{3,2,1,0:T(8,128)(2,1)} %tiles_hbm.1, s32[1,8]{1,0:T(1,128)} %mask_ref.1), custom_call_target="tpu_custom_call" | custom-call | flops 2147483648 | bytes 4194304 | tf_op jit(solution)/shard_map/pallas_call | solution.py:713
  65.3 1.9 %shard_map.77 = (bf16[512,256]{1,0:T(8,128)(2,1)}, bf16[512,256]{1,0:T(8,128)(2,1)}, f32[256,256]{1,0:T(8,128)}) custom-call(bf16[512,256]{1,0:T(8,128)(2,1)} %get-tuple-element.6.act, bf16[512,256]{1,0:T(8,128)(2,1)} %get-tuple-element.7.fg, f32[256,256]{1,0:T(8,128)} %get-tuple-element.8.wg), custom_call_target="tpu_custom_call" | custom-call | bytes 1572864 | tf_op jit(solution)/shard_map/pallas_call | solution.py:760

commit v8 on v7

--- a/solution.py
+++ b/solution.py
@@ -433,8 +433,6 @@
             if f > 0:
                 unfold_copy(f - 1).start()
 
-    weight_steps = 2 * folds + 2
-
     ws[...] = jnp.dot(
         st[pl.ds(pl.multiple_of(c * quarter, quarter), quarter), :], ax[...],
         preferred_element_type=F32,
@@ -515,6 +513,11 @@
         def _():
             relay_partner(k - 4)
 
+        for f in range(folds):
+            @pl.when(k == 8 * f + 6)
+            def _():
+                weight_step(f)
+
         return carry
 
     lax.fori_loop(0, domains + 4, backward_step, 0)
@@ -572,12 +575,12 @@
     for r in range(2):
         part_copy(r).wait_send()
 
-    stages = max(layers + 1, (weight_steps + 1) // 2)
+    stages = max(layers + 1, folds + 3)
     for t in range(stages):
         if t < layers:
             stage_a(t)
-        if 2 * t < weight_steps:
-            weight_step(2 * t)
+        if 1 <= t <= folds + 2:
+            weight_step(folds + t - 1)
         if t + 2 < layers:
             b_copy(target_layer(t + 2), 1 - a).start()
             b_copy(target_layer(t + 2), a).start()
@@ -587,9 +590,6 @@
             stage_relay(0)
         if 2 <= t <= layers:
             stage_relay(t - 1)
-        if 2 * t + 1 < weight_steps:
-            weight_step(2 * t + 1)
-
     w_last = copy_to(w_full.at[c], w_full.at[c], last_send.at[0], last_recv.at[0], d, other)
     w_last.start()
 

time: 67.4 us -> 66.2 us (0.982)
  Pallas kernels: 66.6 us -> 65.4 us
    pallas_call x1, Pallas kernels: 64.7 us -> 63.5 us  [kernel_shards(): pl.pallas_call(functools.partial(layer_kernel, domains, float((rows * dom...]
where the time goes in v8:
time: 66.2 us; the launch traced here: 66 us
  Pallas kernels  65.4 us (99%)
    pallas_call x1, Pallas kernels, kernel_shards(): pl.pallas_call(functools.partial(layer_kernel, domains, float((rows * dom...  63.5 us
    pallas_call x1, Pallas kernels, kernel_shards(): pl.pallas_call(finish_kernel, out_shape=out_shape, in_specs=anywhere, out...  1.88 us

profile of v8, /device:TPU:1, one launch (start us, length us, event | category | flops | bytes accessed | tf_op | source)
XLA Modules:
  0.0 66.0 jit_solution(12914564659481321701)
XLA Ops:
  0.6 63.5 %shard_map.76 = (bf16[512,256]{1,0:T(8,128)(2,1)}, bf16[512,256]{1,0:T(8,128)(2,1)}, f32[256,256]{1,0:T(8,128)}) custom-call(bf16[512,256]{1,0:T(8,128)(2,1)} %x_hbm.1, bf16[256,256]{1,0:T(8,128)(2,1)} %w_hbm.1, bf16[512,256]{1,0:T(8,128)(2,1)} %g_hbm.1, bf16[1,8,512,512]{3,2,1,0:T(8,128)(2,1)} %tiles_hbm.1, s32[1,8]{1,0:T(1,128)} %mask_ref.1), custom_call_target="tpu_custom_call" | custom-call | flops 2147483648 | bytes 4194304 | tf_op jit(solution)/shard_map/pallas_call | solution.py:713
  64.1 1.9 %shard_map.77 = (bf16[512,256]{1,0:T(8,128)(2,1)}, bf16[512,256]{1,0:T(8,128)(2,1)}, f32[256,256]{1,0:T(8,128)}) custom-call(bf16[512,256]{1,0:T(8,128)(2,1)} %get-tuple-element.6.act, bf16[512,256]{1,0:T(8,128)(2,1)} %get-tuple-element.7.fg, f32[256,256]{1,0:T(8,128)} %get-tuple-element.8.wg), custom_call_target="tpu_custom_call" | custom-call | bytes 1572864 | tf_op jit(solution)/shard_map/pallas_call | solution.py:760

commit v9 on v8

--- a/solution.py
+++ b/solution.py
@@ -84,7 +84,7 @@
     domains, scaling,
     x_hbm, w_hbm, g_hbm, tiles_hbm, mask_ref,
     act_hbm, fg_hbm, wg_hbm,
-    act_ref, wg_ref, w_ref, g_ref, tiles, xs, ps, from_b, from_a, from_z, part, part_in, ax, st, ws, w_in, w_cross, w_cross_in, w_full, fg_half,
+    act_ref, wg_ref, w_ref, g_ref, tiles, xs, ps, from_b, from_a, from_z, part, part_out, part_in, ax, st, ws, w_in, w_cross, w_cross_in, w_full, fg_half,
     own_sem, tile_sem, out_sem, x_recv, x_recv_p, x_send_z, x_send_a, x_send_b, x_send_p,
     y_send, y_recv, y_send_z, y_recv_z, y_send_p, y_recv_p,
     part_send, part_recv,
@@ -363,15 +363,16 @@
     lax.fori_loop(1, visits + 5, gather_step, 0)
 
     def part_copy(r):
-        return copy_to(part.at[r], part_in.at[r], part_send.at[r], part_recv.at[r], d, other)
+        return copy_to(part_out.at[r], part_in.at[r], part_send.at[r], part_recv.at[r], d, other)
 
     for r in range(2):
+        part_out[r] = part[r].astype(BF16)
         part_copy(r).start()
 
     for r in range(2):
         part_copy(r).wait_recv()
         rows = pl.ds(r * half, half)
-        ax_here = (part[r] + part_in[r]).astype(BF16)
+        ax_here = (part_out[r].astype(F32) + part_in[r].astype(F32)).astype(BF16)
         ax[rows, :] = ax_here
         total = jnp.dot(ax_here, w_ref[...], preferred_element_type=F32)
         gate = jax.nn.sigmoid(total)
@@ -727,7 +728,8 @@
             pltpu.VMEM((layers, hidden, half), BF16),
             pltpu.VMEM((2, layers, hidden, half), BF16),
             pltpu.VMEM((2, half, hidden), F32),
-            pltpu.VMEM((2, half, hidden), F32),
+            pltpu.VMEM((2, half, hidden), BF16),
+            pltpu.VMEM((2, half, hidden), BF16),
             pltpu.VMEM((rows, hidden), BF16),
             pltpu.VMEM((hidden, rows), BF16),
             pltpu.VMEM((quarter, hidden), F32),

time: 66.2 us -> 65.9 us (level)
  no operation moved by 1% of the time
where the time goes in v9:
time: 65.9 us; the launch traced here: 65.7 us
  Pallas kernels  65.1 us (99%)
    pallas_call x1, Pallas kernels, kernel_shards(): pl.pallas_call(functools.partial(layer_kernel, domains, float((rows * dom...  63.2 us
    pallas_call x1, Pallas kernels, kernel_shards(): pl.pallas_call(finish_kernel, out_shape=out_shape, in_specs=anywhere, out...  1.88 us

profile of v9, /device:TPU:1, one launch (start us, length us, event | category | flops | bytes accessed | tf_op | source)
XLA Modules:
  0.0 65.7 jit_solution(14221865920964484930)
XLA Ops:
  0.6 63.2 %shard_map.76 = (bf16[512,256]{1,0:T(8,128)(2,1)}, bf16[512,256]{1,0:T(8,128)(2,1)}, f32[256,256]{1,0:T(8,128)}) custom-call(bf16[512,256]{1,0:T(8,128)(2,1)} %x_hbm.1, bf16[256,256]{1,0:T(8,128)(2,1)} %w_hbm.1, bf16[512,256]{1,0:T(8,128)(2,1)} %g_hbm.1, bf16[1,8,512,512]{3,2,1,0:T(8,128)(2,1)} %tiles_hbm.1, s32[1,8]{1,0:T(1,128)} %mask_ref.1), custom_call_target="tpu_custom_call" | custom-call | flops 2147483648 | bytes 4194304 | tf_op jit(solution)/shard_map/pallas_call | solution.py:714
  63.8 1.9 %shard_map.77 = (bf16[512,256]{1,0:T(8,128)(2,1)}, bf16[512,256]{1,0:T(8,128)(2,1)}, f32[256,256]{1,0:T(8,128)}) custom-call(bf16[512,256]{1,0:T(8,128)(2,1)} %get-tuple-element.6.act, bf16[512,256]{1,0:T(8,128)(2,1)} %get-tuple-element.7.fg, f32[256,256]{1,0:T(8,128)} %get-tuple-element.8.wg), custom_call_target="tpu_custom_call" | custom-call | bytes 1572864 | tf_op jit(solution)/shard_map/pallas_call | solution.py:762

commit v10 on v9

--- a/solution.py
+++ b/solution.py
@@ -490,7 +490,7 @@
                 ).astype(BF16)
             p_copy(j).start()
 
-            @pl.when(jnp.logical_and(b_ != b, k < 8))
+            @pl.when(jnp.logical_and(b_ != b, k < 12))
             def _():
                 b_copy(z_, a_).start()
 
@@ -501,7 +501,7 @@
         def _():
             copy_to(ps.at[j, c], ps.at[j, c], p_send_p.at[j], p_recv_p.at[j], d, other).wait_recv()
 
-            @pl.when(jnp.logical_and(b_ != b, k < 8))
+            @pl.when(jnp.logical_and(b_ != b, k < 12))
             def _():
                 b_copy(z_, a_).start()
 
@@ -582,9 +582,9 @@
             stage_a(t)
         if 1 <= t <= folds + 2:
             weight_step(folds + t - 1)
-        if t + 2 < layers:
-            b_copy(target_layer(t + 2), 1 - a).start()
-            b_copy(target_layer(t + 2), a).start()
+        if t + 3 < layers:
+            b_copy(target_layer(t + 3), 1 - a).start()
+            b_copy(target_layer(t + 3), a).start()
         if 1 <= t <= layers:
             stage_z(t - 1)
         if t == 2:

time: 65.9 us -> 69.4 us (1.053)
  Pallas kernels: 65.1 us -> 68.6 us
    pallas_call x1, Pallas kernels: 63.2 us -> 66.7 us  [kernel_shards(): pl.pallas_call(functools.partial(layer_kernel, domains, float((rows * dom...]
where the time goes in v10:
time: 69.4 us; the launch traced here: 69.2 us
  Pallas kernels  68.6 us (99%)
    pallas_call x1, Pallas kernels, kernel_shards(): pl.pallas_call(functools.partial(layer_kernel, domains, float((rows * dom...  66.7 us
    pallas_call x1, Pallas kernels, kernel_shards(): pl.pallas_call(finish_kernel, out_shape=out_shape, in_specs=anywhere, out...  1.88 us

profile of v10, /device:TPU:1, one launch (start us, length us, event | category | flops | bytes accessed | tf_op | source)
XLA Modules:
  0.0 69.2 jit_solution(12459091797649889639)
XLA Ops:
  0.6 66.7 %shard_map.76 = (bf16[512,256]{1,0:T(8,128)(2,1)}, bf16[512,256]{1,0:T(8,128)(2,1)}, f32[256,256]{1,0:T(8,128)}) custom-call(bf16[512,256]{1,0:T(8,128)(2,1)} %x_hbm.1, bf16[256,256]{1,0:T(8,128)(2,1)} %w_hbm.1, bf16[512,256]{1,0:T(8,128)(2,1)} %g_hbm.1, bf16[1,8,512,512]{3,2,1,0:T(8,128)(2,1)} %tiles_hbm.1, s32[1,8]{1,0:T(1,128)} %mask_ref.1), custom_call_target="tpu_custom_call" | custom-call | flops 2147483648 | bytes 4194304 | tf_op jit(solution)/shard_map/pallas_call | solution.py:714
  67.3 1.9 %shard_map.77 = (bf16[512,256]{1,0:T(8,128)(2,1)}, bf16[512,256]{1,0:T(8,128)(2,1)}, f32[256,256]{1,0:T(8,128)}) custom-call(bf16[512,256]{1,0:T(8,128)(2,1)} %get-tuple-element.6.act, bf16[512,256]{1,0:T(8,128)(2,1)} %get-tuple-element.7.fg, f32[256,256]{1,0:T(8,128)} %get-tuple-element.8.wg), custom_call_target="tpu_custom_call" | custom-call | bytes 1572864 | tf_op jit(solution)/shard_map/pallas_call | solution.py:762
